TPU v7x, 32 devices: a whole 2x2x4 slice. The times are simulated.
32 devices in a mesh: member: 4 (over z), lat: 8 (over y, x, core).
Axes of the slice: x: 2, y: 2, z: 4, core: 2. Of those that a mesh axis runs over, the one named last changes fastest.
Arguments:
- ensemble_state: float32 [3, 256, 64, 256], P(None, 'member', 'lat'), may hold values from -6 to 6
- obs_cell: int32 [8, 4, 256], replicated, may hold values from 0 to 511
- obs_value: float32 [8, 4, 256], replicated, may hold values from -6 to 6
- obs_prec: float32 [8, 4, 256], replicated, may hold values from 0.5 to 4
Outputs:
- analysis_a: float32 [3, 256, 64, 256], P(None, 'member', 'lat')
Inputs may be any that keep to these rules, and one draw needn't show every extreme that they name: `obs_cell`: each entry is a cell of its patch of 8 by 64 cells, counted row by row.
All inputs are finite; a program needn't handle non-finite values.
Results may differ from a plain program's by a relative error of at most 0.0003.
Values sent between devices are 32-bit elements; how exact they have to be, the bound alone decides.
No kernel may reach another device: no remote copies, remote signals or barrier semaphores. Data moves between devices by JAX's collectives and lax.ppermute only.
A program may use at most 128 MiB of HBM per device.

v0:
```python
import functools

import jax
import jax.numpy as jnp
from jax import lax
from jax.experimental import pallas as pl
from jax.experimental.pallas import tpu as pltpu
from jax.sharding import PartitionSpec as P

ITERS = 12
STEPS = 2
HALO = 2 * STEPS
LANES = 128

time_step = 0.3
coriolis_base = 0.5
coriolis_slope = 1.0

F32 = jnp.float32
BF16 = jnp.bfloat16


def call(kernel, outs, *args, name, flops=0, limit=24, far_in=False, far_out=False):
    shapes = [jax.ShapeDtypeStruct(s, F32) for s in outs[0]]
    spaces = [pl.ANY if far else pltpu.VMEM for far in (far_in, far_out)]
    bytes_moved = sum(a.size * 4 for a in args) + sum(s.size * 4 for s in shapes)
    return pl.pallas_call(
        kernel,
        out_shape=shapes,
        in_specs=[pl.BlockSpec(memory_space=spaces[0])] * len(args),
        out_specs=[pl.BlockSpec(memory_space=spaces[1])] * len(shapes),
        scratch_shapes=outs[1],
        compiler_params=pltpu.CompilerParams(vmem_limit_bytes=limit * 2**20),
        cost_estimate=pl.CostEstimate(flops=flops, bytes_accessed=bytes_moved, transcendentals=0),
        name=name,
    )(*args)


def split(x):
    high = x.astype(BF16)
    return high, (x - high.astype(F32)).astype(BF16)


def dot3(a, b, dims=(((1,), (0,)), ((), ()))):
    ah, al = a
    bh, bl = b
    dot = functools.partial(lax.dot_general, dimension_numbers=dims, preferred_element_type=F32)
    return dot(ah, bh) + (dot(ah, bl) + dot(al, bh))


def model_kernel(source, own, h_pair, h_cross, uv_pair, uv_cross, state, sems):
    _, rows, members, lon = own.shape
    tiles = lon // LANES
    copies = [
        pltpu.make_async_copy(source.at[:, :, pl.ds(t * LANES, LANES)], state.at[t], sems.at[t])
        for t in range(tiles)
    ]
    for copy in copies:
        copy.start()
    lat = lax.axis_index("lat")
    size = lax.axis_size("lat")
    even = lat % 2 == 0
    inside_up = (lat > 0).astype(F32)
    inside_down = (lat < size - 1).astype(F32)
    total = float(rows * size)
    lane = lax.broadcasted_iota(jnp.int32, (8, LANES), 1)
    first, last = lane == 0, lane == LANES - 1
    spins = [
        coriolis_base + coriolis_slope * ((lat * rows + r).astype(F32) / total - 0.5)
        for r in range(-HALO, rows + HALO)
    ]

    def diff_lon(x):
        right = [pltpu.roll(t, 1, 1) for t in x]
        left = [pltpu.roll(t, LANES - 1, 1) for t in x]
        out = []
        for t in range(tiles):
            before = jnp.where(first, right[t - 1] if t else 0.0, right[t])
            after = jnp.where(last, left[t + 1] if t + 1 < tiles else 0.0, left[t])
            out.append(after - before)
        return out

    def block(b, _):
        start = pl.multiple_of(b * 8, 8)

        def load(f, r):
            return [
                state[t, f, pl.ds(start * rows + r, 8, stride=rows), :]
                for t in range(tiles)
            ]

        base = {r: [load(f, r) for f in range(3)] for r in range(rows)}
        y = dict(base)
        for step, factor in enumerate((time_step / 4, time_step / 2, time_step, 2 * time_step)):
            new = {}
            for r in range(-step - 1, rows + step + 1):
                scale = factor
                if r < 0:
                    scale = factor * inside_up
                elif r >= rows:
                    scale = factor * inside_down
                half = 0.5 * scale
                turn = scale * spins[r + HALO]
                here, below, above = y.get(r), y.get(r - 1), y.get(r + 1)
                rates = [[None] * tiles for _ in range(3)]

                def add(f, t, term):
                    rates[f][t] = term if rates[f][t] is None else rates[f][t] + term

                if here is not None:
                    slope_h, slope_u = diff_lon(here[0]), diff_lon(here[1])
                for t in range(tiles):
                    d_v = d_h = None
                    if above is not None and below is not None:
                        d_h, d_v = above[0][t] - below[0][t], above[2][t] - below[2][t]
                    elif above is not None:
                        d_h, d_v = above[0][t], above[2][t]
                    elif below is not None:
                        d_h, d_v = -below[0][t], -below[2][t]
                    if here is not None:
                        d_v = slope_u[t] if d_v is None else d_v + slope_u[t]
                        add(1, t, turn * here[2][t] - half * slope_h[t])
                    if d_v is not None:
                        add(0, t, -half * d_v)
                    if d_h is not None:
                        add(2, t, -half * d_h)
                    if here is not None:
                        add(2, t, -turn * here[1][t])
                zero = jnp.zeros((8, LANES), F32)
                for f in range(3):
                    for t in range(tiles):
                        if r in base:
                            rates[f][t] = base[r][f][t] + rates[f][t]
                        elif rates[f][t] is None:
                            rates[f][t] = zero
                new[r] = rates
            y = new
        at = pl.ds(start, 8)
        for t in range(tiles):
            cols = pl.ds(t * LANES, LANES)
            for r in range(rows):
                for f in range(3):
                    own[f, r, at, cols] = y[r][f][t]
            for i in range(HALO):
                up, down = y[i - HALO], y[rows + i]
                h_pair[i, at, cols] = jnp.where(even, down[0][t], up[0][t])
                h_cross[i, at, cols] = jnp.where(even, up[0][t], down[0][t])
                for f in range(2):
                    uv_pair[f, i, at, cols] = jnp.where(even, down[f + 1][t], up[f + 1][t])
                    uv_cross[f, i, at, cols] = jnp.where(even, up[f + 1][t], down[f + 1][t])
        return 0

    for copy in copies:
        copy.wait()
    lax.fori_loop(0, members // 8, block, 0)


def halo_places(rows):
    even = lax.axis_index("lat") % 2 == 0
    pair = jnp.where(even, rows - HALO, 0)
    return pair, rows - HALO - pair


def observe_kernel(width, own, got_pair, got_cross, cells_row, cells_lane, raw, height):
    _, rows, members, lon = own.shape
    patches, _, n_obs = raw.shape
    pair, cross = halo_places(rows)
    height[...] = own[0]
    height[pl.ds(pair, HALO)] += got_pair[...]
    height[pl.ds(cross, HALO)] += got_cross[...]
    for q in range(patches):
        window = pl.ds(q * width // LANES * LANES, LANES)
        for c in range(0, n_obs, LANES):
            lane = jnp.broadcast_to(cells_lane[q, :, pl.ds(c, LANES)], (members, LANES))
            row = jnp.broadcast_to(cells_row[q, :, pl.ds(c, LANES)], (members, LANES))
            total = None
            for r in range(rows):
                taken = jnp.take_along_axis(height[r, :, window], lane, axis=1)
                total = taken if total is None else jnp.where(row == r, taken, total)
            raw[q, :, pl.ds(c, LANES)] = total


def pack_kernel(width, own, height, got_pair, got_cross, *outs):
    uv = outs[-1]
    outs = outs[:-1]
    _, rows, members, lon = own.shape
    pair, cross = halo_places(rows)
    uv[...] = own[1:3]
    for f in range(2):
        uv[f, pl.ds(pair, HALO)] += got_pair[f]
        uv[f, pl.ds(cross, HALO)] += got_cross[f]
    mine = lax.axis_index("member")
    n = len(outs)
    per = LANES // width
    slot = lax.broadcasted_iota(jnp.int32, (members, LANES), 1) // width
    for s, out in enumerate(outs):
        q = owner_of(mine, s, n)
        start = pl.multiple_of(q * width // LANES * LANES, LANES)
        offset = q * width - start
        for f in range(3):
            source = height if f == 0 else uv.at[f - 1]
            for r in range(0, rows, per):
                total = None
                for i in range(per):
                    line = source[r + i, :, pl.ds(start, LANES)]
                    line = pltpu.roll(line, lax.rem(i * width - offset + LANES, LANES), 1)
                    total = line if total is None else jnp.where(slot == i, line, total)
                out[:, pl.ds((f * rows + r) * width, LANES)] = total


def owner_of(mine, shift, n):
    if n & (n - 1) == 0:
        return mine ^ shift
    return lax.rem(mine + shift, n)


def source_of(mine, shift, n):
    if n & (n - 1) == 0:
        return mine ^ shift
    return lax.rem(mine - shift + n, n)


def swap_links(n, shift):
    return [(i, owner_of(i, shift, n) if n & (n - 1) == 0 else (i + shift) % n) for i in range(n)]


def neighbour_links(n, first):
    links = [(i, i + 1) for i in range(first, n - 1, 2)]
    return links + [(j, i) for i, j in links]


def centred(raw):
    mean = jnp.sum(raw, axis=0, keepdims=True) * (1.0 / raw.shape[0])
    return raw - mean, mean


def gram_kernel(targets, raw_own, raw_pair, raw_cross, weight, value, *outs):
    members, n_obs = raw_own.shape
    total = [None] * len(targets)
    for b, raw in enumerate((raw_own, raw_pair, raw_cross)):
        dev, mean = centred(raw[...])
        innovation = value[b : b + 1] - mean
        right = split(dev)
        for i, t in enumerate(targets):
            w = weight[t, b : b + 1]
            left = jnp.concatenate(
                [dev * w, jnp.broadcast_to(innovation * w, (16, n_obs))], axis=0
            )
            part = dot3(split(left), right, (((1,), (1,)), ((), ())))
            total[i] = part if total[i] is None else total[i] + part
    for out, t in zip(outs, total):
        out[...] = t


def weights_kernel(own, got_pair, got_cross, out):
    members = own.shape[1]
    rows = lax.broadcasted_iota(jnp.int32, (members, members), 0)
    cols = lax.broadcasted_iota(jnp.int32, (members, members), 1)
    diagonal = rows == cols
    at = pl.ds(0, members)
    gram = own[at] + got_pair[at] + got_cross[at]
    gram = gram + jnp.where(diagonal, members - 1.0, 0.0)
    at = pl.ds(members, 8)
    drive = own[at] + got_pair[at] + got_cross[at]
    square = jnp.sum(jnp.sum(gram * gram, axis=0, keepdims=True), axis=1, keepdims=True)
    fro = jnp.sqrt(square)
    root = gram / fro
    inverse = None
    for sweep in range(ITERS):
        root_s = split(root)
        if inverse is None:
            product = root
        else:
            inverse_s = split(inverse)
            product = dot3(inverse_s, root_s)
        correction = jnp.where(diagonal, 1.5, 0.0) - 0.5 * product
        correction_s = split(correction)
        if sweep + 1 < ITERS:
            root = dot3(root_s, correction_s)
        inverse = correction if inverse is None else dot3(correction_s, inverse_s)
    inverse_s = split(inverse)
    mean_weight = dot3(split(dot3(split(drive), inverse_s)), inverse_s)[0:1] / fro
    weights = jnp.sqrt(members - 1.0) / jnp.sqrt(fro) * inverse + mean_weight
    sums = jnp.sum(weights, axis=1, keepdims=True)
    out[...] = weights + (1.0 - sums) * (1.0 / members)


def apply_kernel(n, weights, *refs):
    parts, outs, whole = refs[:n], refs[n : 2 * n], refs[2 * n]
    members = weights.shape[0]
    local, cells = parts[0].shape
    mine = lax.axis_index("member")
    for s, part in enumerate(parts):
        whole[pl.ds(pl.multiple_of(source_of(mine, s, n) * local, local), local), :] = part[...]
    wide = 2 * LANES
    for c in range(0, cells, wide):
        at = pl.ds(c, wide)
        field = split(whole[:, at])
        for s, out in enumerate(outs):
            k = pl.multiple_of(source_of(mine, s, n) * local, local)
            out[:, at] = dot3(split(weights[pl.ds(k, local), :]), field)


def unpack_kernel(width, n, rows, *refs):
    parts, (out, whole, lines_out, sems) = refs[:n], refs[n:]
    members = parts[0].shape[0]
    mine = lax.axis_index("member")
    for s, part in enumerate(parts):
        whole[owner_of(mine, s, n)] = part[...]
    per = LANES // width
    slot = lax.broadcasted_iota(jnp.int32, (members, LANES), 1) // width
    copies = []
    for f in range(3):
        for r in range(0, rows, per):
            cols = pl.ds((f * rows + r) * width, LANES)
            for t in range(n // per):
                lines = [whole[t * per + i, :, cols] for i in range(per)]
                for j in range(per):
                    total = None
                    for i in range(per):
                        line = lines[i]
                        if i != j:
                            line = pltpu.roll(line, (i - j) * width % LANES, 1)
                        total = line if total is None else jnp.where(slot == i, line, total)
                    lines_out[t, f, pl.ds(r + j, members, stride=rows), :] = total
        for t in range(n // per):
            copies.append(
                pltpu.make_async_copy(
                    lines_out.at[t, f], out.at[f, :, pl.ds(t * LANES, LANES)], sems.at[t, f]
                )
            )
            copies[-1].start()
    for copy in copies:
        copy.wait()


def body(ensemble_state, obs_cell, obs_value, obs_prec):
    _, members, rows, lon = ensemble_state.shape
    n_lat, n_member = lax.axis_size("lat"), lax.axis_size("member")
    lat, mine = lax.axis_index("lat"), lax.axis_index("member")
    width = lon // n_member
    all_members = members * n_member
    patches, n_obs = obs_cell.shape[1:]
    zero = jnp.zeros((), jnp.int32)
    pair_lat, cross_lat = neighbour_links(n_lat, 0), neighbour_links(n_lat, 1)
    pair_lon, cross_lon = neighbour_links(n_member, 0), neighbour_links(n_member, 1)

    offsets = jnp.arange(3, dtype=jnp.int32) - 1

    def near(array):
        padded = jnp.pad(array, ((0, 0), (1, 1), (0, 0)))
        return lax.dynamic_slice(padded, (lat, mine, zero), (1, 3, n_obs))[0]

    def ordered(array, index, axis):
        low, middle, high = [lax.index_in_dim(array, i, axis, keepdims=True) for i in range(3)]
        even = index % 2 == 0
        return jnp.concatenate(
            [middle, jnp.where(even, high, low), jnp.where(even, low, high)], axis=axis
        )

    cells = near(obs_cell)
    obs_row = (-offsets[:, None, None] * rows + cells // width).astype(F32)
    obs_col = (offsets[:, None] * width + cells % width).astype(F32)
    north = (obs_row - 0.5 * (rows - 1)) / rows
    east = (obs_col - 0.5 * (width - 1)) / width
    weight = near(obs_prec) * jnp.exp(-0.5 * (north * north + east * east))
    weight = ordered(ordered(weight, mine, 1), lat, 0)
    value = ordered(near(obs_value), mine, 0)
    band = lax.dynamic_slice(obs_cell, (lat, zero, zero), (1, patches, n_obs))[0][:, None, :]
    starts = jnp.arange(patches, dtype=jnp.int32)[:, None, None] * width % LANES
    cells_row, cells_lane = band // width, band % width + starts

    edge = (HALO, members, lon)
    own, h_pair, h_cross, uv_pair, uv_cross = call(
        model_kernel,
        (
            [(3, rows, members, lon), edge, edge, (2,) + edge, (2,) + edge],
            [
                pltpu.VMEM((lon // LANES, 3, members * rows, LANES), F32),
                pltpu.SemaphoreType.DMA((lon // LANES,)),
            ],
        ),
        ensemble_state.reshape(3, members * rows, lon),
        name="model",
        far_in=True,
    )
    got_cross = lax.ppermute(h_cross, "lat", cross_lat)
    got_pair = lax.ppermute(h_pair, "lat", pair_lat)
    raw, height = call(
        functools.partial(observe_kernel, width),
        ([(patches, members, n_obs), (rows, members, lon)], []),
        own,
        got_pair,
        got_cross,
        cells_row,
        cells_lane,
        name="observe",
    )
    raw = lax.all_to_all(raw, "member", split_axis=0, concat_axis=0, tiled=True)
    raw = raw.reshape(all_members, n_obs)
    uv_cross, uv_pair = lax.ppermute(uv_cross, "lat", cross_lat), lax.ppermute(uv_pair, "lat", pair_lat)
    packed = call(
        functools.partial(pack_kernel, width),
        ([(members, 3 * rows * width)] * n_member, [pltpu.VMEM((2, rows, members, lon), F32)]),
        own,
        height,
        uv_pair,
        uv_cross,
        name="pack",
    )
    raw_cross = lax.ppermute(raw, "member", cross_lon)
    raw_pair = lax.ppermute(raw, "member", pair_lon)
    order = sorted(range(1, n_member), key=lambda s: (-(s & -s), s))
    parts = [packed[0]] + [None] * (n_member - 1)
    for s in order:
        parts[s] = lax.ppermute(packed[s], "member", swap_links(n_member, s))
    gram_shape = (all_members + 16, all_members)
    flops = 2 * 9 * all_members**2 * n_obs
    gram_cross, gram_pair = call(
        functools.partial(gram_kernel, (2, 1)),
        ([gram_shape] * 2, []),
        raw, raw_pair, raw_cross, weight, value,
        name="gram_beside", flops=2 * flops,
    )
    gram_cross = lax.ppermute(gram_cross, "lat", cross_lat)
    gram_pair = lax.ppermute(gram_pair, "lat", pair_lat)
    (gram_own,) = call(
        functools.partial(gram_kernel, (0,)),
        ([gram_shape], []),
        raw, raw_pair, raw_cross, weight, value,
        name="gram_own", flops=flops,
    )
    (weights,) = call(
        weights_kernel,
        ([(all_members, all_members)], []),
        gram_own, gram_pair, gram_cross,
        name="weights", flops=2 * 9 * 12 * all_members**3,
    )
    shape = packed[0].shape
    done = call(
        functools.partial(apply_kernel, n_member),
        ([shape] * n_member, [pltpu.VMEM((all_members, shape[1]), F32)]),
        weights, *parts,
        name="apply", flops=6 * all_members**2 * shape[1],
    )
    final = [done[0]] + [None] * (n_member - 1)
    for s in order:
        back = [(j, i) for i, j in swap_links(n_member, s)]
        final[s] = lax.ppermute(done[s], "member", back)
    (analysis,) = call(
        functools.partial(unpack_kernel, width, n_member, rows),
        (
            [(3, members * rows, lon)],
            [
                pltpu.VMEM((n_member,) + shape, F32),
                pltpu.VMEM((lon // LANES, 3, members * rows, LANES), F32),
                pltpu.SemaphoreType.DMA((lon // LANES, 3)),
            ],
        ),
        *final,
        name="unpack",
        far_out=True,
    )
    return analysis.reshape(ensemble_state.shape)


def solution(mesh):
    in_specs = (P(None, "member", "lat", None), P(), P(), P())
    out_specs = P(None, "member", "lat", None)
    return jax.shard_map(body, mesh=mesh, in_specs=in_specs, out_specs=out_specs, check_vma=False)
```

profile of v0, /device:TPU:11, one launch (start us, length us, event | category | flops | bytes accessed | tf_op | source)
XLA Modules:
  0.0 122.9 jit_solution(2719542205090304224)
XLA Ops:
  0.0 0.0 copy-start
  0.0 1.4 %copy-done = f32[3,64,8,256]{3,2,1,0:T(8,128)S(1)} copy-done((f32[3,64,8,256]{3,2,1,0:T(8,128)S(1)}, f32[3,64,8,256]{3,2,1,0:T(8,128)}, u32[]{:S(2)}) %copy-start) | copy-done | bytes 1572888
  1.4 0.0 copy-start.4
  1.4 0.0 copy-start.5
  1.4 4.6 %model.1 = (f32[3,8,64,256]{3,2,1,0:T(8,128)S(1)}, f32[4,64,256]{2,1,0:T(8,128)}, f32[4,64,256]{2,1,0:T(8,128)S(1)}, f32[2,4,64,256]{3,2,1,0:T(8,128)}, f32[2,4,64,256]{3,2,1,0:T(8,128)}) custom-call(f32[3,512,256]{2,1,0:T(8,128)S(1)} %bitcast.15), custom_call_target="tpu_custom_call" | custom-call | bytes 4718592 | tf_op jit(solution)/shard_map/model/pallas_call | solution.py:27
  6.0 0.0 copy-start.6
  6.0 0.7 collective-permute-start
  6.8 3.0 %collective-permute-start.1 = (f32[4,64,256]{2,1,0:T(8,128)S(1)}, f32[4,64,256]{2,1,0:T(8,128)S(1)}, u32[]{:S(2)}, u32[]{:S(2)}) collective-permute-start(f32[4,64,256]{2,1,0:T(8,128)S(1)} %get-tuple-element.24), channel_id=1, source_target_pairs={{1,2},{3,4},{5,6},{2,1},{4,3},{6,5},{9,10},{11,12},{13,14},{10,9},... | collective-permute-start | bytes 786440 | tf_op jit(solution)/shard_map/ppermute | solution.py:387
  9.8 0.1 collective-permute-start.6
  9.9 3.5 %collective-permute-start.7 = (f32[2,4,64,256]{3,2,1,0:T(8,128)}, f32[2,4,64,256]{3,2,1,0:T(8,128)S(1)}, u32[]{:S(2)}, u32[]{:S(2)}) collective-permute-start(f32[2,4,64,256]{3,2,1,0:T(8,128)} %get-tuple-element.30), channel_id=1, source_target_pairs={{1,2},{3,4},{5,6},{2,1},{4,3},{6,5},{9,10},{11,12},{13,14},{10,9},... | collective-permute-start | bytes 1572872 | tf_op jit(solution)/shard_map/ppermute | solution.py:401
  13.4 0.0 copy-done.4
  13.5 0.0 copy-done.5
  13.5 0.1 fusion.6
  13.6 0.1 fusion.7
  13.7 0.1 exponential_multiply_fusion
  13.8 0.0 collective-permute-done.got_pair
  13.8 4.3 %collective-permute-done.1.got_cross = f32[4,64,256]{2,1,0:T(8,128)S(1)} collective-permute-done((f32[4,64,256]{2,1,0:T(8,128)S(1)}, f32[4,64,256]{2,1,0:T(8,128)S(1)}, u32[]{:S(2)}, u32[]{:S(2)}) %collective-permute-start.1) | collective-permute-done | bytes 262176 | tf_op jit(solution)/shard_map/ppermute | solution.py:387
  18.1 0.0 copy-start.2
  18.1 0.7 copy-done.2
  18.8 0.0 copy-start.3
  18.8 0.9 copy-done.3
  19.8 0.8 observe.1
  20.5 0.0 copy-start.1
  20.5 0.7 copy-done.1
  21.2 4.8 %all-to-all-start = ((f32[4,64,256]{2,1,0:T(8,128)}), f32[4,64,256]{2,1,0:T(8,128)S(1)}, u32[]{:S(2)}, u32[]{:S(2)}) async-start(f32[4,64,256]{2,1,0:T(8,128)} %copy-done.1), calls=%async_computation | async-start | bytes 524288 | tf_op jit(solution)/shard_map/all_to_all | solution.py:399
  26.0 0.0 copy-done.6
  26.1 5.9 %all-to-all-done = f32[4,64,256]{2,1,0:T(8,128)S(1)} async-done(((f32[4,64,256]{2,1,0:T(8,128)}), f32[4,64,256]{2,1,0:T(8,128)S(1)}, u32[]{:S(2)}, u32[]{:S(2)}) %all-to-all-start) | async-done | bytes 262176 | tf_op jit(solution)/shard_map/all_to_all | solution.py:399
  31.9 2.0 %collective-permute-start.3 = (f32[256,256]{1,0:T(8,128)S(1)}, f32[256,256]{1,0:T(8,128)S(1)}, u32[]{:S(2)}, u32[]{:S(2)}) collective-permute-start(f32[256,256]{1,0:T(8,128)S(1)} %bitcast.16), channel_id=1, source_target_pairs={{8,16},{16,8},{9,17},{17,9},{10,18},{18,10},{11,19},{19,11},{12,20... | collective-permute-start | bytes 786440 | tf_op jit(solution)/shard_map/ppermute | solution.py:411
  33.9 0.3 collective-permute-start.2
  34.3 7.3 %collective-permute-done.3.raw_cross = f32[256,256]{1,0:T(8,128)S(1)} collective-permute-done((f32[256,256]{1,0:T(8,128)S(1)}, f32[256,256]{1,0:T(8,128)S(1)}, u32[]{:S(2)}, u32[]{:S(2)}) %collective-permute-start.3) | collective-permute-done | bytes 262176 | tf_op jit(solution)/shard_map/ppermute | solution.py:411
  41.6 0.4 collective-permute-done.2.raw_pair
  42.0 0.9 gram_beside.1
  42.9 0.8 collective-permute-start.4
  43.7 1.9 %collective-permute-start.5 = (f32[272,256]{1,0:T(8,128)S(1)}, f32[272,256]{1,0:T(8,128)S(1)}, u32[]{:S(2)}, u32[]{:S(2)}) collective-permute-start(f32[272,256]{1,0:T(8,128)S(1)} %get-tuple-element.27), channel_id=1, source_target_pairs={{1,2},{3,4},{5,6},{2,1},{4,3},{6,5},{9,10},{11,12},{13,14},{10,9},... | collective-permute-start | bytes 835592 | tf_op jit(solution)/shard_map/ppermute | solution.py:425
  45.6 0.0 collective-permute-done.6.got_pair
  45.6 0.0 collective-permute-done.7.got_cross
  45.6 1.0 pack.1
  46.6 0.1 collective-permute-start.8
  46.7 2.5 %collective-permute-start.9 = (f32[64,1536]{1,0:T(8,128)S(1)}, f32[64,1536]{1,0:T(8,128)S(1)}, u32[]{:S(2)}, u32[]{:S(2)}) collective-permute-start(f32[64,1536]{1,0:T(8,128)S(1)} %get-tuple-element.33), channel_id=1, source_target_pairs={{0,16},{8,24},{16,0},{24,8},{1,17},{9,25},{17,1},{25,9},{2,18},{10... | collective-permute-start | bytes 1179656 | tf_op jit(solution)/shard_map/ppermute | solution.py:416
  49.2 0.1 collective-permute-start.10
  49.3 0.6 gram_own.1.own
  49.9 0.0 collective-permute-done.4.got_pair
  49.9 3.3 %collective-permute-done.5.got_cross = f32[272,256]{1,0:T(8,128)S(1)} collective-permute-done((f32[272,256]{1,0:T(8,128)S(1)}, f32[272,256]{1,0:T(8,128)S(1)}, u32[]{:S(2)}, u32[]{:S(2)}) %collective-permute-start.5) | collective-permute-done | bytes 278560 | tf_op jit(solution)/shard_map/ppermute | solution.py:425
  53.3 8.1 %weights.1 = f32[256,256]{1,0:T(8,128)S(1)} custom-call(f32[272,256]{1,0:T(8,128)S(1)} %gram_own.1.own, f32[272,256]{1,0:T(8,128)S(1)} %collective-permute-done.4.got_pair, f32[272,256]{1,0:T(8,128)S(1)} %collective-permute-done.5.got_cross), custom_call_target="tpu_custom_call" | custom-call | flops 3623878656 | bytes 1097728 | tf_op jit(solution)/shard_map/weights/pallas_call | solution.py:27
  61.3 2.0 %collective-permute-done.8.refs_1_ = f32[64,1536]{1,0:T(8,128)S(1)} collective-permute-done((f32[64,1536]{1,0:T(8,128)S(1)}, f32[64,1536]{1,0:T(8,128)S(1)}, u32[]{:S(2)}, u32[]{:S(2)}) %collective-permute-start.8) | collective-permute-done | bytes 393248 | tf_op jit(solution)/shard_map/ppermute | solution.py:416
  63.4 11.4 %collective-permute-done.9.refs_2_ = f32[64,1536]{1,0:T(8,128)S(1)} collective-permute-done((f32[64,1536]{1,0:T(8,128)S(1)}, f32[64,1536]{1,0:T(8,128)S(1)}, u32[]{:S(2)}, u32[]{:S(2)}) %collective-permute-start.9) | collective-permute-done | bytes 393248 | tf_op jit(solution)/shard_map/ppermute | solution.py:416
  74.8 8.8 %collective-permute-done.10.refs_3_ = f32[64,1536]{1,0:T(8,128)S(1)} collective-permute-done((f32[64,1536]{1,0:T(8,128)S(1)}, f32[64,1536]{1,0:T(8,128)S(1)}, u32[]{:S(2)}, u32[]{:S(2)}) %collective-permute-start.10) | collective-permute-done | bytes 393248 | tf_op jit(solution)/shard_map/ppermute | solution.py:416
  83.6 1.9 %apply.1 = (f32[64,1536]{1,0:T(8,128)S(1)}, f32[64,1536]{1,0:T(8,128)S(1)}, f32[64,1536]{1,0:T(8,128)S(1)}, f32[64,1536]{1,0:T(8,128)S(1)}) custom-call(f32[256,256]{1,0:T(8,128)S(1)} %weights.1, f32[64,1536]{1,0:T(8,128)S(1)} %get-tuple-element.31.refs_0_, f32[64,1536]{1,0:T(8,128)S(1)} %collective-permute-done.8.refs_1_, ...), custom_call_target="tpu_custom_call" | custom-call | flops 603979776 | bytes 3407872 | tf_op jit(solution)/shard_map/apply/pallas_call | solution.py:27
  85.5 0.1 collective-permute-start.11
  85.5 3.0 %collective-permute-start.12 = (f32[64,1536]{1,0:T(8,128)S(1)}, f32[64,1536]{1,0:T(8,128)S(1)}, u32[]{:S(2)}, u32[]{:S(2)}) collective-permute-start(f32[64,1536]{1,0:T(8,128)S(1)} %get-tuple-element.37), channel_id=1, source_target_pairs={{16,0},{24,8},{0,16},{8,24},{17,1},{25,9},{1,17},{9,25},{18,2},{26... | collective-permute-start | bytes 1179656 | tf_op jit(solution)/shard_map/ppermute | solution.py:449
  88.5 0.0 collective-permute-start.13
  88.5 12.3 %collective-permute-done.11.refs_1_ = f32[64,1536]{1,0:T(8,128)S(1)} collective-permute-done((f32[64,1536]{1,0:T(8,128)S(1)}, f32[64,1536]{1,0:T(8,128)S(1)}, u32[]{:S(2)}, u32[]{:S(2)}) %collective-permute-start.11) | collective-permute-done | bytes 393248 | tf_op jit(solution)/shard_map/ppermute | solution.py:449
  100.8 4.7 %collective-permute-done.12.refs_2_ = f32[64,1536]{1,0:T(8,128)S(1)} collective-permute-done((f32[64,1536]{1,0:T(8,128)S(1)}, f32[64,1536]{1,0:T(8,128)S(1)}, u32[]{:S(2)}, u32[]{:S(2)}) %collective-permute-start.12) | collective-permute-done | bytes 393248 | tf_op jit(solution)/shard_map/ppermute | solution.py:449
  105.5 15.9 %collective-permute-done.13.refs_3_ = f32[64,1536]{1,0:T(8,128)S(1)} collective-permute-done((f32[64,1536]{1,0:T(8,128)S(1)}, f32[64,1536]{1,0:T(8,128)S(1)}, u32[]{:S(2)}, u32[]{:S(2)}) %collective-permute-start.13) | collective-permute-done | bytes 393248 | tf_op jit(solution)/shard_map/ppermute | solution.py:449
  121.4 1.5 %unpack.1 = f32[3,512,256]{2,1,0:T(8,128)} custom-call(f32[64,1536]{1,0:T(8,128)S(1)} %get-tuple-element.35.refs_0_, f32[64,1536]{1,0:T(8,128)S(1)} %collective-permute-done.11.refs_1_, f32[64,1536]{1,0:T(8,128)S(1)} %collective-permute-done.12.refs_2_, f32[64,1536]{1,0:T(8,128)S(1)} %collective-permute-done.13.refs_3_), custom_call_target="tpu_custom_call" | custom-call | bytes 3145728 | tf_op jit(solution)/shard_map/unpack/pallas_call | solution.py:27
  (13 shorter events, 0.1 us)
Async XLA Ops:
  0.0 1.4 %copy-start = (f32[3,64,8,256]{3,2,1,0:T(8,128)S(1)}, f32[3,64,8,256]{3,2,1,0:T(8,128)}, u32[]{:S(2)}) copy-start(f32[3,64,8,256]{3,2,1,0:T(8,128)} %param.4) | copy-start | bytes 4718596
  1.4 12.0 %copy-start.4 = (s32[8,4,256]{2,1,0:T(4,128)S(1)}, s32[8,4,256]{2,1,0:T(4,128)}, u32[]{:S(2)}) copy-start(s32[8,4,256]{2,1,0:T(4,128)} %param.5) | copy-start | bytes 98308
  1.4 12.1 %copy-start.5 = (f32[8,4,256]{2,1,0:T(4,128)S(1)}, f32[8,4,256]{2,1,0:T(4,128)}, u32[]{:S(2)}) copy-start(f32[8,4,256]{2,1,0:T(4,128)} %param.7) | copy-start | bytes 98308
  6.0 20.0 %copy-start.6 = (f32[8,4,256]{2,1,0:T(4,128)S(1)}, f32[8,4,256]{2,1,0:T(4,128)}, u32[]{:S(2)}) copy-start(f32[8,4,256]{2,1,0:T(4,128)} %param.6) | copy-start | bytes 98308
  6.0 7.8 %collective-permute-start = (f32[4,64,256]{2,1,0:T(8,128)}, f32[4,64,256]{2,1,0:T(8,128)S(1)}, u32[]{:S(2)}, u32[]{:S(2)}) collective-permute-start(f32[4,64,256]{2,1,0:T(8,128)} %get-tuple-element.23), channel_id=1, source_target_pairs={{0,1},{2,3},{4,5},{6,7},{1,0},{3,2},{5,4},{7,6},{8,9},{10,11},{12,... | collective-permute-start | bytes 786440 | tf_op jit(solution)/shard_map/ppermute | solution.py:388
  6.8 11.3 %collective-permute-start.1 = (f32[4,64,256]{2,1,0:T(8,128)S(1)}, f32[4,64,256]{2,1,0:T(8,128)S(1)}, u32[]{:S(2)}, u32[]{:S(2)}) collective-permute-start(f32[4,64,256]{2,1,0:T(8,128)S(1)} %get-tuple-element.24), channel_id=1, source_target_pairs={{1,2},{3,4},{5,6},{2,1},{4,3},{6,5},{9,10},{11,12},{13,14},{10,9},... | collective-permute-start | bytes 786440 | tf_op jit(solution)/shard_map/ppermute | solution.py:387
  9.8 35.8 %collective-permute-start.6 = (f32[2,4,64,256]{3,2,1,0:T(8,128)}, f32[2,4,64,256]{3,2,1,0:T(8,128)S(1)}, u32[]{:S(2)}, u32[]{:S(2)}) collective-permute-start(f32[2,4,64,256]{3,2,1,0:T(8,128)} %get-tuple-element.29), channel_id=1, source_target_pairs={{0,1},{2,3},{4,5},{6,7},{1,0},{3,2},{5,4},{7,6},{8,9},{10,11},{12,... | collective-permute-start | bytes 1572872 | tf_op jit(solution)/shard_map/ppermute | solution.py:401
  9.9 35.7 %collective-permute-start.7 = (f32[2,4,64,256]{3,2,1,0:T(8,128)}, f32[2,4,64,256]{3,2,1,0:T(8,128)S(1)}, u32[]{:S(2)}, u32[]{:S(2)}) collective-permute-start(f32[2,4,64,256]{3,2,1,0:T(8,128)} %get-tuple-element.30), channel_id=1, source_target_pairs={{1,2},{3,4},{5,6},{2,1},{4,3},{6,5},{9,10},{11,12},{13,14},{10,9},... | collective-permute-start | bytes 1572872 | tf_op jit(solution)/shard_map/ppermute | solution.py:401
  18.1 0.7 copy-start.2
  18.8 0.9 copy-start.3
  20.5 0.7 copy-start.1
  21.2 10.7 %all-to-all-start = ((f32[4,64,256]{2,1,0:T(8,128)}), f32[4,64,256]{2,1,0:T(8,128)S(1)}, u32[]{:S(2)}, u32[]{:S(2)}) async-start(f32[4,64,256]{2,1,0:T(8,128)} %copy-done.1), calls=%async_computation | async-start | bytes 524288 | tf_op jit(solution)/shard_map/all_to_all | solution.py:399
  31.9 9.6 %collective-permute-start.3 = (f32[256,256]{1,0:T(8,128)S(1)}, f32[256,256]{1,0:T(8,128)S(1)}, u32[]{:S(2)}, u32[]{:S(2)}) collective-permute-start(f32[256,256]{1,0:T(8,128)S(1)} %bitcast.16), channel_id=1, source_target_pairs={{8,16},{16,8},{9,17},{17,9},{10,18},{18,10},{11,19},{19,11},{12,20... | collective-permute-start | bytes 786440 | tf_op jit(solution)/shard_map/ppermute | solution.py:411
  33.9 8.1 %collective-permute-start.2 = (f32[256,256]{1,0:T(8,128)S(1)}, f32[256,256]{1,0:T(8,128)S(1)}, u32[]{:S(2)}, u32[]{:S(2)}) collective-permute-start(f32[256,256]{1,0:T(8,128)S(1)} %bitcast.17), channel_id=1, source_target_pairs={{0,8},{16,24},{8,0},{24,16},{1,9},{17,25},{9,1},{25,17},{2,10},{18... | collective-permute-start | bytes 786440 | tf_op jit(solution)/shard_map/ppermute | solution.py:412
  42.9 7.0 %collective-permute-start.4 = (f32[272,256]{1,0:T(8,128)S(1)}, f32[272,256]{1,0:T(8,128)S(1)}, u32[]{:S(2)}, u32[]{:S(2)}) collective-permute-start(f32[272,256]{1,0:T(8,128)S(1)} %get-tuple-element.26), channel_id=1, source_target_pairs={{0,1},{2,3},{4,5},{6,7},{1,0},{3,2},{5,4},{7,6},{8,9},{10,11},{12,... | collective-permute-start | bytes 835592 | tf_op jit(solution)/shard_map/ppermute | solution.py:426
  43.7 9.6 %collective-permute-start.5 = (f32[272,256]{1,0:T(8,128)S(1)}, f32[272,256]{1,0:T(8,128)S(1)}, u32[]{:S(2)}, u32[]{:S(2)}) collective-permute-start(f32[272,256]{1,0:T(8,128)S(1)} %get-tuple-element.27), channel_id=1, source_target_pairs={{1,2},{3,4},{5,6},{2,1},{4,3},{6,5},{9,10},{11,12},{13,14},{10,9},... | collective-permute-start | bytes 835592 | tf_op jit(solution)/shard_map/ppermute | solution.py:425
  46.6 16.7 %collective-permute-start.8 = (f32[64,1536]{1,0:T(8,128)S(1)}, f32[64,1536]{1,0:T(8,128)S(1)}, u32[]{:S(2)}, u32[]{:S(2)}) collective-permute-start(f32[64,1536]{1,0:T(8,128)S(1)} %get-tuple-element.32), channel_id=1, source_target_pairs={{0,8},{8,0},{16,24},{24,16},{1,9},{9,1},{17,25},{25,17},{2,10},{10... | collective-permute-start | bytes 1179656 | tf_op jit(solution)/shard_map/ppermute | solution.py:416
  46.7 28.1 %collective-permute-start.9 = (f32[64,1536]{1,0:T(8,128)S(1)}, f32[64,1536]{1,0:T(8,128)S(1)}, u32[]{:S(2)}, u32[]{:S(2)}) collective-permute-start(f32[64,1536]{1,0:T(8,128)S(1)} %get-tuple-element.33), channel_id=1, source_target_pairs={{0,16},{8,24},{16,0},{24,8},{1,17},{9,25},{17,1},{25,9},{2,18},{10... | collective-permute-start | bytes 1179656 | tf_op jit(solution)/shard_map/ppermute | solution.py:416
  49.2 34.4 %collective-permute-start.10 = (f32[64,1536]{1,0:T(8,128)S(1)}, f32[64,1536]{1,0:T(8,128)S(1)}, u32[]{:S(2)}, u32[]{:S(2)}) collective-permute-start(f32[64,1536]{1,0:T(8,128)S(1)} %get-tuple-element.34), channel_id=1, source_target_pairs={{0,24},{8,16},{16,8},{24,0},{1,25},{9,17},{17,9},{25,1},{2,26},{10... | collective-permute-start | bytes 1179656 | tf_op jit(solution)/shard_map/ppermute | solution.py:416
  85.5 15.3 %collective-permute-start.11 = (f32[64,1536]{1,0:T(8,128)S(1)}, f32[64,1536]{1,0:T(8,128)S(1)}, u32[]{:S(2)}, u32[]{:S(2)}) collective-permute-start(f32[64,1536]{1,0:T(8,128)S(1)} %get-tuple-element.36), channel_id=1, source_target_pairs={{8,0},{0,8},{24,16},{16,24},{9,1},{1,9},{25,17},{17,25},{10,2},{2,... | collective-permute-start | bytes 1179656 | tf_op jit(solution)/shard_map/ppermute | solution.py:449
  85.5 20.0 %collective-permute-start.12 = (f32[64,1536]{1,0:T(8,128)S(1)}, f32[64,1536]{1,0:T(8,128)S(1)}, u32[]{:S(2)}, u32[]{:S(2)}) collective-permute-start(f32[64,1536]{1,0:T(8,128)S(1)} %get-tuple-element.37), channel_id=1, source_target_pairs={{16,0},{24,8},{0,16},{8,24},{17,1},{25,9},{1,17},{9,25},{18,2},{26... | collective-permute-start | bytes 1179656 | tf_op jit(solution)/shard_map/ppermute | solution.py:449
  88.5 32.8 %collective-permute-start.13 = (f32[64,1536]{1,0:T(8,128)S(1)}, f32[64,1536]{1,0:T(8,128)S(1)}, u32[]{:S(2)}, u32[]{:S(2)}) collective-permute-start(f32[64,1536]{1,0:T(8,128)S(1)} %get-tuple-element.38), channel_id=1, source_target_pairs={{24,0},{16,8},{8,16},{0,24},{25,1},{17,9},{9,17},{1,25},{26,2},{18... | collective-permute-start | bytes 1179656 | tf_op jit(solution)/shard_map/ppermute | solution.py:449
where the time goes:
time: 125 us; the launch traced here: 123 us
  waiting for transfers between devices  76.3 us (61%)
  starting transfers between devices  22.8 us (18%)
  Pallas kernels  19.3 us (15%)
  local copies, waits for them, and re-layouts  3.78 us (3%)
    ppermute x3, waiting for transfers between devices, body(): final[s] = lax.ppermute(done[s], 'member', back)  32.8 us
    ppermute x3, waiting for transfers between devices, body(): parts[s] = lax.ppermute(packed[s], 'member', swap_links(n_member, s))  22.2 us
    pallas_call x8, Pallas kernels, call(): pl.pallas_call(kernel, out_shape=shapes, in_specs=[pl.BlockSpec(memory_sp...  19.3 us
    ppermute x1, waiting for transfers between devices, body(): raw_cross = lax.ppermute(raw, 'member', cross_lon)  7.3 us
    all_to_all x1, waiting for transfers between devices, body(): raw = lax.all_to_all(raw, 'member', split_axis=0, concat_axis=0, tiled=True)  5.88 us
    all_to_all x1, starting transfers between devices, body(): raw = lax.all_to_all(raw, 'member', split_axis=0, concat_axis=0, tiled=True)  4.76 us
    ppermute x1, waiting for transfers between devices, body(): got_cross = lax.ppermute(h_cross, 'lat', cross_lat)  4.29 us
    unnamed x14, local copies, waits for them, and re-layouts  3.78 us
  transfers between devices with their start and end apart: 15, of which 11 were waited for; matrix products, arithmetic and copies ran while one was open for 0% of the time, Pallas kernels for 9%

commit v1 on v0

v1 whole, which is shorter than its diff:
```python
import functools

import jax
import jax.numpy as jnp
from jax import lax
from jax.experimental import pallas as pl
from jax.experimental.pallas import tpu as pltpu
from jax.sharding import PartitionSpec as P

ITERS = 12
STEPS = 2
HALO = 2 * STEPS
LANES = 128
LIMIT = 12

time_step = 0.3
coriolis_base = 0.5
coriolis_slope = 1.0

F32 = jnp.float32
BF16 = jnp.bfloat16


def call(kernel, outs, *args, name, flops=0, limit=LIMIT):
    shapes = [jax.ShapeDtypeStruct(s, F32) for s in outs[0]]
    bytes_moved = 0
    return pl.pallas_call(
        kernel,
        out_shape=shapes,
        in_specs=[pl.BlockSpec(memory_space=pltpu.VMEM)] * len(args),
        out_specs=[pl.BlockSpec(memory_space=pltpu.VMEM)] * len(shapes),
        scratch_shapes=outs[1],
        compiler_params=pltpu.CompilerParams(vmem_limit_bytes=limit * 2**20),
        cost_estimate=pl.CostEstimate(flops=0, bytes_accessed=bytes_moved, transcendentals=0),
        name=name,
    )(*args)


def split(x):
    high = x.astype(BF16)
    return high, (x - high.astype(F32)).astype(BF16)


def dot3(a, b, dims=(((1,), (0,)), ((), ()))):
    ah, al = a
    bh, bl = b
    dot = functools.partial(lax.dot_general, dimension_numbers=dims, preferred_element_type=F32)
    return dot(ah, bh) + (dot(ah, bl) + dot(al, bh))


def coefficients(rows):
    lat, size = lax.axis_index("lat"), lax.axis_size("lat")
    inside_up = (lat > 0).astype(F32)
    inside_down = (lat < size - 1).astype(F32)
    inside = {r: inside_up if r < 0 else inside_down for r in range(-HALO, rows + HALO)}
    spins = {
        r: coriolis_base + coriolis_slope * ((lat * rows + r).astype(F32) / float(rows * size) - 0.5)
        for r in inside
    }
    return inside, spins


def integrate(base, diff_lon, keep, rows, inside, spins):
    tiles = len(base[0][0])
    y = dict(base)
    for step, factor in enumerate((time_step / 4, time_step / 2, time_step, 2 * time_step)):
        new = {}
        for r in range(-step - 1, rows + step + 1):
            scale = factor if 0 <= r < rows else factor * inside[r]
            half, turn = 0.5 * scale, scale * spins[r]
            if keep is not None:
                half, turn = half * keep, turn * keep
            here, below, above = y.get(r), y.get(r - 1), y.get(r + 1)
            rates = [[None] * tiles for _ in range(3)]

            def add(f, t, term):
                rates[f][t] = term if rates[f][t] is None else rates[f][t] + term

            if here is not None:
                slope_h, slope_u = diff_lon(here[0]), diff_lon(here[1])
            for t in range(tiles):
                d_v = d_h = None
                if above is not None and below is not None:
                    d_h, d_v = above[0][t] - below[0][t], above[2][t] - below[2][t]
                elif above is not None:
                    d_h, d_v = above[0][t], above[2][t]
                elif below is not None:
                    d_h, d_v = -below[0][t], -below[2][t]
                if here is not None:
                    d_v = slope_u[t] if d_v is None else d_v + slope_u[t]
                    add(1, t, turn * here[2][t] - half * slope_h[t])
                if d_v is not None:
                    add(0, t, -half * d_v)
                if d_h is not None:
                    add(2, t, -half * d_h)
                if here is not None:
                    add(2, t, -turn * here[1][t])
            for f in range(3):
                for t in range(tiles):
                    if r in base:
                        rates[f][t] = base[r][f][t] + rates[f][t]
                    elif rates[f][t] is None:
                        rates[f][t] = jnp.zeros((8, LANES), F32)
            new[r] = rates
        y = new
    return y


def model_kernel(state, own, h_pair, h_cross, uv_pair, uv_cross):
    _, rows, members, lon = own.shape
    tiles = lon // LANES
    even = lax.axis_index("lat") % 2 == 0
    inside, spins = coefficients(rows)
    lane = lax.broadcasted_iota(jnp.int32, (8, LANES), 1)
    first, last = lane == 0, lane == LANES - 1

    def diff_lon(x):
        right = [pltpu.roll(t, 1, 1) for t in x]
        left = [pltpu.roll(t, LANES - 1, 1) for t in x]
        out = []
        for t in range(tiles):
            before = jnp.where(first, right[t - 1] if t else 0.0, right[t])
            after = jnp.where(last, left[t + 1] if t + 1 < tiles else 0.0, left[t])
            out.append(after - before)
        return out

    def block(b, _):
        start = pl.multiple_of(b * 8, 8)

        def load(f, r):
            return [
                state[f, pl.ds((start * tiles + t) * rows + r, 8, stride=rows * tiles), :]
                for t in range(tiles)
            ]

        base = {r: [load(f, r) for f in range(3)] for r in range(rows)}
        y = integrate(base, diff_lon, None, rows, inside, spins)
        at = pl.ds(start, 8)
        for t in range(tiles):
            cols = pl.ds(t * LANES, LANES)
            for r in range(rows):
                for f in range(3):
                    own[f, r, at, cols] = y[r][f][t]
            for i in range(HALO):
                up, down = y[i - HALO], y[rows + i]
                h_pair[i, at, cols] = jnp.where(even, down[0][t], up[0][t])
                h_cross[i, at, cols] = jnp.where(even, up[0][t], down[0][t])
                for f in range(2):
                    uv_pair[f, i, at, cols] = jnp.where(even, down[f + 1][t], up[f + 1][t])
                    uv_cross[f, i, at, cols] = jnp.where(even, up[f + 1][t], down[f + 1][t])
        return 0

    lax.fori_loop(0, members // 8, block, 0)


def early_kernel(width, n, shift, rows, state, out):
    members = out.shape[0]
    tiles = state.shape[1] // members // rows
    q = owner_of(lax.axis_index("member"), shift, n)
    per = LANES // width
    lane = lax.broadcasted_iota(jnp.int32, (members, LANES), 1)
    slot = lane // width

    def line(f, r, tile):
        return state[f, pl.ds(tile * rows + r, members, stride=rows * tiles), :]

    tile = q * width // LANES
    offset = q * width - tile * LANES
    left = jnp.maximum(q * width - HALO, 0)
    right = jnp.minimum(q * width + width, tiles * LANES - HALO)
    left_tile, right_tile = left // LANES, right // LANES
    left_off, right_off = left - left_tile * LANES, right - right_tile * LANES
    has_left, has_right = q > 0, q < n - 1
    total = None
    for g in range(3 * rows):
        f, r = g // rows, g % rows
        i = r % per
        piece = pltpu.roll(line(f, r, tile), lax.rem(i * width - offset + LANES, LANES), 1)
        body = piece if i == 0 else jnp.where(slot == i, piece, body)
        if i == per - 1:
            out[:, pl.ds((g - i) * width, LANES)] = body
        at = g * 2 * HALO % LANES
        if at == 0:
            total = jnp.zeros((members, LANES), F32)
        piece = pltpu.roll(line(f, r, left_tile), lax.rem(at - left_off + LANES, LANES), 1)
        total = jnp.where((lane >= at) & (lane < at + HALO) & has_left, piece, total)
        at = at + HALO
        piece = pltpu.roll(line(f, r, right_tile), lax.rem(at - right_off + LANES, LANES), 1)
        total = jnp.where((lane >= at) & (lane < at + HALO) & has_right, piece, total)
        if at + HALO == LANES or g == 3 * rows - 1:
            first = 3 * rows * width + g * 2 * HALO // LANES * LANES
            out[:, pl.ds(first, LANES)] = total


def owner_model_kernel(width, n, rows, block_in, own, to_pair, to_cross):
    members = own.shape[0]
    per = LANES // width
    q = lax.axis_index("member")
    even = lax.axis_index("lat") % 2 == 0
    inside, spins = coefficients(rows)
    lane = lax.broadcasted_iota(jnp.int32, (8, LANES), 1)
    slot = lane // width
    middle = (LANES + width) // 2
    mine = (lane < width).astype(F32)
    on_right = ((lane >= width) & (lane < middle)).astype(F32) * (q < n - 1).astype(F32)
    on_left = (lane >= middle).astype(F32) * (q > 0).astype(F32)
    keep = mine + on_right + on_left

    def diff_lon(x):
        return [pltpu.roll(t, LANES - 1, 1) - pltpu.roll(t, 1, 1) for t in x]

    def dense(lines):
        total = lines[0]
        for i in range(1, per):
            total = jnp.where(slot == i, pltpu.roll(lines[i], i * width, 1), total)
        return total

    def block(b, _):
        at = pl.ds(pl.multiple_of(b * 8, 8), 8)
        base = {r: [None] * 3 for r in range(rows)}
        for g in range(3 * rows):
            f, r = g // rows, g % rows
            i = r % per
            body = block_in[at, pl.ds((g - i) * width, LANES)]
            if i:
                body = pltpu.roll(body, LANES - i * width, 1)
            place = g * 2 * HALO
            edge = block_in[at, pl.ds(3 * rows * width + place // LANES * LANES, LANES)]
            place = place % LANES
            left = pltpu.roll(edge, (LANES - HALO - place) % LANES, 1)
            right = pltpu.roll(edge, (width - HALO - place) % LANES, 1)
            row = jnp.where(lane < width, body, 0.0)
            row = jnp.where((lane >= width) & (lane < width + HALO), right, row)
            base[r][f] = [jnp.where(lane >= LANES - HALO, left, row)]
        y = integrate(base, diff_lon, keep, rows, inside, spins)
        for f in range(3):
            for r in range(0, rows, per):
                lines = [y[r + i][f][0] for i in range(per)]
                own[at, pl.ds((f * rows + r) * width, LANES)] = dense(lines)
            for i in range(0, HALO, per):
                up = dense([y[i + j - HALO][f][0] for j in range(per)])
                down = dense([y[rows + i + j][f][0] for j in range(per)])
                cols = pl.ds((f * HALO + i) * width, LANES)
                to_pair[at, cols] = jnp.where(even, down, up)
                to_cross[at, cols] = jnp.where(even, up, down)
        return 0

    lax.fori_loop(0, members // 8, block, 0)


def halo_places(rows):
    even = lax.axis_index("lat") % 2 == 0
    pair = jnp.where(even, rows - HALO, 0)
    return pair, rows - HALO - pair


def pick(array, lat, q):
    rows = array[lat].astype(F32)
    chosen = lax.broadcasted_iota(jnp.int32, rows.shape, 0) == q
    return jnp.sum(jnp.where(chosen, rows, 0.0), axis=0, keepdims=True)


def observe_kernel(width, own, got_pair, got_cross, cells, seen, height):
    _, rows, members, lon = own.shape
    patches, _, n_obs = seen.shape
    pair, cross = halo_places(rows)
    height[...] = own[0]
    height[pl.ds(pair, HALO)] += got_pair[...]
    height[pl.ds(cross, HALO)] += got_cross[...]
    for q in range(patches):
        start = q * width // LANES * LANES
        window = pl.ds(start, LANES)
        picked = pick(cells, lax.axis_index("lat"), q)
        for c in range(0, n_obs, LANES):
            cell = picked[:, c : c + LANES]
            row = jnp.floor((cell + 0.5) * (1.0 / width))
            lane = (cell - row * width).astype(jnp.int32) + (q * width - start)
            lane = jnp.broadcast_to(lane, (members, LANES))
            row = jnp.broadcast_to(row.astype(jnp.int32), (members, LANES))
            total = None
            for r in range(rows):
                taken = jnp.take_along_axis(height[r, :, window], lane, axis=1)
                total = taken if total is None else jnp.where(row == r, taken, total)
            seen[q, :, pl.ds(c, LANES)] = total


def pack_kernel(width, n, shifts, own, height, got_pair, got_cross, *refs):
    *outs, wind = refs
    _, rows, members, lon = own.shape
    pair, cross = halo_places(rows)
    wind[...] = own[1:3]
    for f in range(2):
        wind[f, pl.ds(pair, HALO)] += got_pair[f]
        wind[f, pl.ds(cross, HALO)] += got_cross[f]
    mine = lax.axis_index("member")
    per = LANES // width
    slot = lax.broadcasted_iota(jnp.int32, (members, LANES), 1) // width
    for s, out in zip(shifts, outs):
        q = owner_of(mine, s, n)
        start = pl.multiple_of(q * width // LANES * LANES, LANES)
        offset = q * width - start
        for f in range(3):
            source = height if f == 0 else wind.at[f - 1]
            for r in range(0, rows, per):
                total = None
                for i in range(per):
                    line = source[r + i, :, pl.ds(start, LANES)]
                    line = pltpu.roll(line, lax.rem(i * width - offset + LANES, LANES), 1)
                    total = line if total is None else jnp.where(slot == i, line, total)
                out[:, pl.ds((f * rows + r) * width, LANES)] = total


def owner_of(mine, shift, n):
    if n & (n - 1) == 0:
        return mine ^ shift
    return lax.rem(mine + shift, n)


def source_of(mine, shift, n):
    if n & (n - 1) == 0:
        return mine ^ shift
    return lax.rem(mine - shift + n, n)


def swap_links(n, shift):
    return [(i, owner_of(i, shift, n) if n & (n - 1) == 0 else (i + shift) % n) for i in range(n)]


def neighbour_links(n, first):
    links = [(i, i + 1) for i in range(first, n - 1, 2)]
    return links + [(j, i) for i, j in links]


def centred(raw):
    mean = jnp.sum(raw, axis=0, keepdims=True) * (1.0 / raw.shape[0])
    return raw - mean, mean


def gram_kernel(which, n, rows, width, cells, values, precs, raw_own, raw_pair, raw_cross, *outs):
    members, n_obs = raw_own.shape
    lat, mine = lax.axis_index("lat"), lax.axis_index("member")
    side = 1 - 2 * lax.rem(mine, 2)
    toward = 1 - 2 * lax.rem(lat, 2)
    total = [None] * len(which)
    for raw, b in ((raw_own, 0 * side), (raw_pair, side), (raw_cross, -side)):
        q = mine + b
        cell = pick(cells, lat, q)
        row = jnp.floor((cell + 0.5) * (1.0 / width))
        col = cell - row * width + (b * width).astype(F32)
        east = (col - 0.5 * (width - 1)) / width
        prec = pick(precs, lat, q)
        dev, mean = centred(raw[...])
        innovation = pick(values, lat, q) - mean
        right = split(dev)
        for i, t in enumerate(which):
            north = (row - (t * toward * rows).astype(F32) - 0.5 * (rows - 1)) / rows
            w = prec * jnp.exp(-0.5 * (north * north + east * east))
            left = jnp.concatenate(
                [dev * w, jnp.broadcast_to(innovation * w, (16, n_obs))], axis=0
            )
            part = dot3(split(left), right, (((1,), (1,)), ((), ())))
            total[i] = part if total[i] is None else total[i] + part
    for out, t in zip(outs, total):
        out[...] = t


def weights_kernel(own, got_pair, got_cross, out):
    members = own.shape[1]
    rows = lax.broadcasted_iota(jnp.int32, (members, members), 0)
    cols = lax.broadcasted_iota(jnp.int32, (members, members), 1)
    diagonal = rows == cols
    at = pl.ds(0, members)
    gram = own[at] + got_pair[at] + got_cross[at]
    gram = gram + jnp.where(diagonal, members - 1.0, 0.0)
    at = pl.ds(members, 8)
    drive = own[at] + got_pair[at] + got_cross[at]
    square = jnp.sum(jnp.sum(gram * gram, axis=0, keepdims=True), axis=1, keepdims=True)
    fro = jnp.sqrt(square)
    root = gram / fro
    inverse = None
    for sweep in range(ITERS):
        root_s = split(root)
        if inverse is None:
            product = root
        else:
            inverse_s = split(inverse)
            product = dot3(inverse_s, root_s)
        correction = jnp.where(diagonal, 1.5, 0.0) - 0.5 * product
        correction_s = split(correction)
        if sweep + 1 < ITERS:
            root = dot3(root_s, correction_s)
        inverse = correction if inverse is None else dot3(correction_s, inverse_s)
    inverse_s = split(inverse)
    mean_weight = dot3(split(dot3(split(drive), inverse_s)), inverse_s)[0:1] / fro
    weights = jnp.sqrt(members - 1.0) / jnp.sqrt(fro) * inverse + mean_weight
    sums = jnp.sum(weights, axis=1, keepdims=True)
    out[...] = weights + (1.0 - sums) * (1.0 / members)


def apply_kernel(n, shifts, early, rows, weights, *refs):
    parts, late, (pair_in, cross_in), outs, whole = (
        refs[: n - 1],
        refs[n - 1],
        refs[n : n + 2],
        refs[n + 2 : 2 * n + 2],
        refs[2 * n + 2],
    )
    local, cells = late.shape
    mine = lax.axis_index("member")

    def place(s):
        return pl.ds(pl.multiple_of(source_of(mine, s, n) * local, local), local)

    for s, part in zip(shifts, parts):
        whole[place(s), :] = part[...]
    at = place(early)
    whole[at, :] = late[...]
    edge = cells // 3 // rows * HALO
    for f in range(3):
        for got, first in zip((pair_in, cross_in), halo_places(rows)):
            start = pl.multiple_of(f * (cells // 3) + first // HALO * edge, edge)
            whole[at, pl.ds(start, edge)] += got[:, pl.ds(f * edge, edge)]
    wide = 2 * LANES
    for c in range(0, cells, wide):
        at = pl.ds(c, wide)
        field = split(whole[:, at])
        for s, out in enumerate(outs):
            k = pl.multiple_of(source_of(mine, s, n) * local, local)
            out[:, at] = dot3(split(weights[pl.ds(k, local), :]), field)


def unpack_kernel(width, n, rows, *refs):
    *parts, out, whole = refs
    members = parts[0].shape[0]
    mine = lax.axis_index("member")
    for s, part in enumerate(parts):
        whole[owner_of(mine, s, n)] = part[...]
    per = LANES // width
    tiles = n // per
    slot = lax.broadcasted_iota(jnp.int32, (members, LANES), 1) // width
    for f in range(3):
        for r in range(0, rows, per):
            cols = pl.ds((f * rows + r) * width, LANES)
            for t in range(tiles):
                lines = [whole[t * per + i, :, cols] for i in range(per)]
                for j in range(per):
                    total = None
                    for i in range(per):
                        line = lines[i]
                        if i != j:
                            line = pltpu.roll(line, (i - j) * width % LANES, 1)
                        total = line if total is None else jnp.where(slot == i, line, total)
                    out[f, pl.ds(t * rows + r + j, members, stride=rows * tiles), :] = total


def after(array, *others):
    return lax.optimization_barrier((array,) + others)[0]


def body(ensemble_state, obs_cell, obs_value, obs_prec):
    _, members, rows, lon = ensemble_state.shape
    n_lat, n_member = lax.axis_size("lat"), lax.axis_size("member")
    width = lon // n_member
    all_members = members * n_member
    n_obs = obs_cell.shape[2]
    pair_lat, cross_lat = neighbour_links(n_lat, 0), neighbour_links(n_lat, 1)
    pair_lon, cross_lon = neighbour_links(n_member, 0), neighbour_links(n_member, 1)

    tiles = lon // LANES
    state = ensemble_state.reshape(3, members, rows, tiles, LANES).transpose(0, 1, 3, 2, 4)
    state = state.reshape(3, members * tiles * rows, LANES)
    early = n_member // 2
    order = sorted(range(1, n_member), key=lambda s: (-(s & -s), s))
    late = [0] + [s for s in order if s != early]
    dense = 3 * rows * width
    halo_lanes = -(-3 * rows * 2 * HALO // LANES) * LANES
    (early_block,) = call(
        functools.partial(early_kernel, width, n_member, early, rows),
        ([(members, dense + halo_lanes)], []),
        state,
        name="early",
    )
    state = after(state, early_block)
    early_block = lax.ppermute(early_block, "member", swap_links(n_member, early))
    edge = (HALO, members, lon)
    own, h_pair, h_cross, uv_pair, uv_cross = call(
        model_kernel,
        ([(3, rows, members, lon), edge, edge, (2,) + edge, (2,) + edge], []),
        state,
        name="model",
    )
    got_cross = lax.ppermute(h_cross, "lat", cross_lat)
    got_pair = lax.ppermute(h_pair, "lat", pair_lat)
    seen, height = call(
        functools.partial(observe_kernel, width),
        ([(n_member, members, n_obs), (rows, members, lon)], []),
        own, got_pair, got_cross, obs_cell,
        name="observe",
    )
    seen = lax.all_to_all(seen, "member", split_axis=0, concat_axis=0, tiled=True)
    uv_cross = lax.ppermute(after(uv_cross, early_block), "lat", cross_lat)
    uv_pair = lax.ppermute(after(uv_pair, early_block), "lat", pair_lat)
    packed = call(
        functools.partial(pack_kernel, width, n_member, late),
        ([(members, dense)] * (n_member - 1), [pltpu.VMEM((2, rows, members, lon), F32)]),
        own, height, uv_pair, uv_cross,
        name="pack",
    )
    parts = [packed[0]] + [
        lax.ppermute(block, "member", swap_links(n_member, s))
        for s, block in zip(late[1:], packed[1:])
    ]
    beside = (members, 3 * HALO * width)
    early_own, early_pair, early_cross = call(
        functools.partial(owner_model_kernel, width, n_member, rows),
        ([(members, dense), beside, beside], []),
        early_block,
        name="owner_model",
    )
    early_cross = lax.ppermute(early_cross, "lat", cross_lat)
    early_pair = lax.ppermute(early_pair, "lat", pair_lat)
    raw = after(seen, early_block).reshape(all_members, n_obs)
    raw_cross = lax.ppermute(raw, "member", cross_lon)
    raw_pair = lax.ppermute(raw, "member", pair_lon)
    raw_cross, raw_pair = lax.optimization_barrier((raw_cross, raw_pair, *packed, early_own))[:2]
    gram_shape = (all_members + 16, all_members)
    sizes, observations = (n_member, rows, width), (obs_cell, obs_value, obs_prec)
    flops = 2 * 9 * all_members**2 * n_obs
    gram_cross, gram_pair = call(
        functools.partial(gram_kernel, (-1, 1), *sizes),
        ([gram_shape] * 2, []),
        *observations, raw, raw_pair, raw_cross,
        name="gram_beside", flops=2 * flops,
    )
    gram_cross = lax.ppermute(gram_cross, "lat", cross_lat)
    gram_pair = lax.ppermute(gram_pair, "lat", pair_lat)
    (gram_own,) = call(
        functools.partial(gram_kernel, (0,), *sizes),
        ([gram_shape], []),
        *observations, raw, raw_pair, raw_cross,
        name="gram_own", flops=flops,
    )
    (weights,) = call(
        weights_kernel,
        ([(all_members, all_members)], []),
        gram_own, gram_pair, gram_cross,
        name="weights", flops=2 * 9 * 12 * all_members**3,
    )
    shape = (members, dense)
    done = call(
        functools.partial(apply_kernel, n_member, late, early, rows),
        ([shape] * n_member, [pltpu.VMEM((all_members, dense), F32)]),
        weights, *parts, early_own, early_pair, early_cross,
        name="apply", flops=6 * all_members**2 * dense,
    )
    final = [done[0]] + [None] * (n_member - 1)
    for s in order:
        back = [(j, i) for i, j in swap_links(n_member, s)]
        final[s] = lax.ppermute(done[s], "member", back)
    (analysis,) = call(
        functools.partial(unpack_kernel, width, n_member, rows),
        ([(3, members * tiles * rows, LANES)], [pltpu.VMEM((n_member,) + shape, F32)]),
        *final,
        name="unpack",
    )
    analysis = analysis.reshape(3, members, tiles, rows, LANES).transpose(0, 1, 3, 2, 4)
    return analysis.reshape(ensemble_state.shape)


def solution(mesh):
    in_specs = (P(None, "member", "lat", None), P(), P(), P())
    out_specs = P(None, "member", "lat", None)
    return jax.shard_map(body, mesh=mesh, in_specs=in_specs, out_specs=out_specs, check_vma=False)
```

time: 125 us -> 110 us (0.88); the launches traced: 123 us -> 109 us
  waiting for transfers between devices: 76.3 us -> 51.3 us
  starting transfers between devices: 22.8 us -> 29.2 us
  Pallas kernels: 19.3 us -> 23.9 us
    ppermute x5 -> x7, waiting for transfers between devices: 22.3 us -> 4.42 us  [the longest x1 4.41 us: body(): uv_cross = lax.ppermute(after(uv_cross, early_block), 'lat', cross_lat)]
    ppermute x1, waiting for transfers between devices: 7.3 us -> 0.01 us  [body(): raw_cross = lax.ppermute(raw, 'member', cross_lon)]
    pallas_call x8 -> x10, Pallas kernels: 19.3 us -> 23.9 us  [call(): pl.pallas_call(kernel, out_shape=shapes, in_specs=[pl.BlockSpec(memory_sp...]
    ppermute x5 -> x7, starting transfers between devices: 6.27 us -> 10.8 us  [the longest x1 3.34 us: body(): uv_cross = lax.ppermute(after(uv_cross, early_block), 'lat', cross_lat)]
    all_to_all x1, waiting for transfers between devices: 5.88 us -> 1.82 us  [body(): lax.all_to_all(seen, 'member', split_axis=0, concat_axis=0, tiled=True)]
    ppermute x1, starting transfers between devices: 1.91 us -> 5.56 us  [body(): gram_cross = lax.ppermute(gram_cross, 'lat', cross_lat)]
    ppermute x1, waiting for transfers between devices: 4.29 us -> 7.74 us  [body(): got_cross = lax.ppermute(h_cross, 'lat', cross_lat)]
    unnamed x14 -> x18, local copies, waits for them, and re-layouts: 3.78 us -> 4.72 us
  transfers between devices with their start and end apart: 15 -> 17, of which waited for: 11 -> 7; matrix products, arithmetic and copies ran while one was open for 0% -> 0% of each run, Pallas kernels for 9% -> 16%
where the time goes in v1:
time: 110 us; the launch traced here: 109 us
  waiting for transfers between devices  51.3 us (47%)
  starting transfers between devices  29.2 us (27%)
  Pallas kernels  23.9 us (22%)
  local copies, waits for them, and re-layouts  4.72 us (4%)
    ppermute x3, waiting for transfers between devices, body(): final[s] = lax.ppermute(done[s], 'member', back)  33.2 us
    pallas_call x10, Pallas kernels, call(): pl.pallas_call(kernel, out_shape=shapes, in_specs=[pl.BlockSpec(memory_sp...  23.9 us
    ppermute x1, waiting for transfers between devices, body(): got_cross = lax.ppermute(h_cross, 'lat', cross_lat)  7.74 us
    ppermute x1, starting transfers between devices, body(): gram_cross = lax.ppermute(gram_cross, 'lat', cross_lat)  5.56 us
    unnamed x18, local copies, waits for them, and re-layouts  4.72 us
    ppermute x1, waiting for transfers between devices, body(): uv_cross = lax.ppermute(after(uv_cross, early_block), 'lat', cross_lat)  4.41 us
    ppermute x1, waiting for transfers between devices, body(): gram_cross = lax.ppermute(gram_cross, 'lat', cross_lat)  4.15 us
    all_to_all x1, starting transfers between devices, body(): lax.all_to_all(seen, 'member', split_axis=0, concat_axis=0, tiled=True)  3.82 us
  transfers between devices with their start and end apart: 17, of which 7 were waited for; matrix products, arithmetic and copies ran while one was open for 0% of the time, Pallas kernels for 16%

profile of v1, /device:TPU:11, one launch (start us, length us, event | category | flops | bytes accessed | tf_op | source)
XLA Modules:
  0.0 109.4 jit_solution(1682865785992563494)
XLA Ops:
  0.0 0.0 copy-start
  0.0 1.4 %copy-done = f32[3,64,8,256]{3,2,1,0:T(8,128)S(1)} copy-done((f32[3,64,8,256]{3,2,1,0:T(8,128)S(1)}, f32[3,64,8,256]{3,2,1,0:T(8,128)}, u32[]{:S(2)}) %copy-start) | copy-done | bytes 1572888
  1.4 0.0 copy-start.3
  1.4 1.2 %early.1 = f32[64,1792]{1,0:T(8,128)S(1)} custom-call(f32[3,1024,128]{2,1,0:T(8,128)S(1)} %bitcast.11), custom_call_target="tpu_custom_call" | custom-call | tf_op jit(solution)/shard_map/early/pallas_call | solution.py:27
  2.6 2.3 %collective-permute-start.2 = (f32[64,1792]{1,0:T(8,128)S(1)}, f32[64,1792]{1,0:T(8,128)S(1)}, u32[]{:S(2)}, u32[]{:S(2)}) collective-permute-start(f32[64,1792]{1,0:T(8,128)S(1)} %early.1), channel_id=1, source_target_pairs={{0,16},{8,24},{16,0},{24,8},{1,17},{9,25},{17,1},{25,9},{2,18},{10... | collective-permute-start | bytes 1376264 | tf_op jit(solution)/shard_map/ppermute | solution.py:484
  4.9 3.4 %model.1 = (f32[3,8,64,256]{3,2,1,0:T(8,128)S(1)}, f32[4,64,256]{2,1,0:T(8,128)S(1)}, f32[4,64,256]{2,1,0:T(8,128)S(1)}, f32[2,4,64,256]{3,2,1,0:T(8,128)S(1)}, f32[2,4,64,256]{3,2,1,0:T(8,128)S(1)}) custom-call(f32[3,1024,128]{2,1,0:T(8,128)S(1)} %bitcast.12), custom_call_target="tpu_custom_call" | custom-call | tf_op jit(solution)/shard_map/model/pallas_call | solution.py:27
  8.4 0.0 copy-start.8
  8.4 0.8 copy-done.8
  9.2 0.0 copy-start.7
  9.2 1.0 collective-permute-start
  10.1 3.0 %collective-permute-start.1 = (f32[4,64,256]{2,1,0:T(8,128)S(1)}, f32[4,64,256]{2,1,0:T(8,128)S(1)}, u32[]{:S(2)}, u32[]{:S(2)}) collective-permute-start(f32[4,64,256]{2,1,0:T(8,128)S(1)} %get-tuple-element.33), channel_id=1, source_target_pairs={{1,2},{3,4},{5,6},{2,1},{4,3},{6,5},{9,10},{11,12},{13,14},{10,9},... | collective-permute-start | bytes 786440 | tf_op jit(solution)/shard_map/ppermute | solution.py:492
  13.1 0.0 collective-permute-done.got_pair
  13.1 7.7 %collective-permute-done.1.got_cross = f32[4,64,256]{2,1,0:T(8,128)S(1)} collective-permute-done((f32[4,64,256]{2,1,0:T(8,128)S(1)}, f32[4,64,256]{2,1,0:T(8,128)S(1)}, u32[]{:S(2)}, u32[]{:S(2)}) %collective-permute-start.1) | collective-permute-done | bytes 262176 | tf_op jit(solution)/shard_map/ppermute | solution.py:492
  20.9 0.0 copy-done.3
  20.9 0.8 observe.1
  21.7 0.0 copy-done.7
  21.7 0.0 copy-start.4
  21.7 0.7 copy-done.4
  22.4 3.8 %all-to-all-start = ((f32[4,64,256]{2,1,0:T(8,128)}), f32[4,64,256]{2,1,0:T(8,128)S(1)}, u32[]{:S(2)}, u32[]{:S(2)}) async-start(f32[4,64,256]{2,1,0:T(8,128)} %copy-done.4), calls=%async_computation | async-start | bytes 524288 | tf_op jit(solution)/shard_map/all_to_all | solution.py:500
  26.2 0.0 collective-permute-done.2.block_in
  26.2 0.0 copy-start.1
  26.2 0.8 copy-done.1
  27.0 0.0 collective-permute-start.5
  27.0 3.3 %collective-permute-start.6 = (f32[2,4,64,256]{3,2,1,0:T(8,128)}, f32[2,4,64,256]{3,2,1,0:T(8,128)S(1)}, u32[]{:S(2)}, u32[]{:S(2)}) collective-permute-start(f32[2,4,64,256]{3,2,1,0:T(8,128)} %copy-done.7), channel_id=1, source_target_pairs={{1,2},{3,4},{5,6},{2,1},{4,3},{6,5},{9,10},{11,12},{13,14},{10,9},... | collective-permute-start | bytes 1572872 | tf_op jit(solution)/shard_map/ppermute | solution.py:501
  30.4 1.8 %all-to-all-done = f32[4,64,256]{2,1,0:T(8,128)S(1)} async-done(((f32[4,64,256]{2,1,0:T(8,128)}), f32[4,64,256]{2,1,0:T(8,128)S(1)}, u32[]{:S(2)}, u32[]{:S(2)}) %all-to-all-start) | async-done | bytes 262176 | tf_op jit(solution)/shard_map/all_to_all | solution.py:500
  32.2 2.0 %collective-permute-start.3 = (f32[256,256]{1,0:T(8,128)S(1)}, f32[256,256]{1,0:T(8,128)S(1)}, u32[]{:S(2)}, u32[]{:S(2)}) collective-permute-start(f32[256,256]{1,0:T(8,128)S(1)} %bitcast.13), channel_id=1, source_target_pairs={{8,16},{16,8},{9,17},{17,9},{10,18},{18,10},{11,19},{19,11},{12,20... | collective-permute-start | bytes 786440 | tf_op jit(solution)/shard_map/ppermute | solution.py:523
  34.1 0.3 collective-permute-start.4
  34.4 0.0 copy-start.2
  34.5 1.0 copy-done.2
  35.5 4.2 %owner_model.1 = (f32[64,1536]{1,0:T(8,128)S(1)}, f32[64,768]{1,0:T(8,128)S(1)}, f32[64,768]{1,0:T(8,128)S(1)}) custom-call(f32[64,1792]{1,0:T(8,128)S(1)} %copy-done.2), custom_call_target="tpu_custom_call" | custom-call | tf_op jit(solution)/shard_map/owner_model/pallas_call | solution.py:27
  39.6 0.0 collective-permute-done.5.got_pair
  39.6 4.4 %collective-permute-done.6.got_cross = f32[2,4,64,256]{3,2,1,0:T(8,128)S(1)} collective-permute-done((f32[2,4,64,256]{3,2,1,0:T(8,128)}, f32[2,4,64,256]{3,2,1,0:T(8,128)S(1)}, u32[]{:S(2)}, u32[]{:S(2)}) %collective-permute-start.6) | collective-permute-done | bytes 524320 | tf_op jit(solution)/shard_map/ppermute | solution.py:501
  44.1 0.0 copy-start.5
  44.1 0.0 copy-start.6
  44.1 0.8 pack.1
  44.9 0.0 collective-permute-done.3.raw_cross
  44.9 0.0 collective-permute-done.4.raw_pair
  44.9 0.0 copy-done.5
  44.9 0.0 copy-done.6
  44.9 0.9 gram_beside.1
  45.8 0.1 collective-permute-start.7
  45.9 0.5 collective-permute-start.10
  46.4 2.3 %collective-permute-start.9 = (f32[64,1536]{1,0:T(8,128)S(1)}, f32[64,1536]{1,0:T(8,128)S(1)}, u32[]{:S(2)}, u32[]{:S(2)}) collective-permute-start(f32[64,1536]{1,0:T(8,128)S(1)} %get-tuple-element.42), channel_id=1, source_target_pairs={{0,8},{8,0},{16,24},{24,16},{1,9},{9,1},{17,25},{25,17},{2,10},{10... | collective-permute-start | bytes 1179656 | tf_op jit(solution)/shard_map/ppermute | solution.py:510
  48.7 5.6 %collective-permute-start.8 = (f32[272,256]{1,0:T(8,128)S(1)}, f32[272,256]{1,0:T(8,128)S(1)}, u32[]{:S(2)}, u32[]{:S(2)}) collective-permute-start(f32[272,256]{1,0:T(8,128)S(1)} %get-tuple-element.48), channel_id=1, source_target_pairs={{1,2},{3,4},{5,6},{2,1},{4,3},{6,5},{9,10},{11,12},{13,14},{10,9},... | collective-permute-start | bytes 835592 | tf_op jit(solution)/shard_map/ppermute | solution.py:535
  54.3 0.1 collective-permute-start.11
  54.4 0.0 collective-permute-done.7.got_pair
  54.4 2.3 %collective-permute-start.12 = (f32[64,768]{1,0:T(8,128)S(1)}, f32[64,768]{1,0:T(8,128)S(1)}, u32[]{:S(2)}, u32[]{:S(2)}) collective-permute-start(f32[64,768]{1,0:T(8,128)S(1)} %get-tuple-element.50), channel_id=1, source_target_pairs={{1,2},{3,4},{5,6},{2,1},{4,3},{6,5},{9,10},{11,12},{13,14},{10,9},... | collective-permute-start | bytes 589832 | tf_op jit(solution)/shard_map/ppermute | solution.py:520
  56.6 0.6 gram_own.1.own
  57.2 4.2 %collective-permute-done.8.got_cross = f32[272,256]{1,0:T(8,128)S(1)} collective-permute-done((f32[272,256]{1,0:T(8,128)S(1)}, f32[272,256]{1,0:T(8,128)S(1)}, u32[]{:S(2)}, u32[]{:S(2)}) %collective-permute-start.8) | collective-permute-done | bytes 278560 | tf_op jit(solution)/shard_map/ppermute | solution.py:535
  61.4 8.0 %weights.1 = f32[256,256]{1,0:T(8,128)S(1)} custom-call(f32[272,256]{1,0:T(8,128)S(1)} %gram_own.1.own, f32[272,256]{1,0:T(8,128)S(1)} %collective-permute-done.7.got_pair, f32[272,256]{1,0:T(8,128)S(1)} %collective-permute-done.8.got_cross), custom_call_target="tpu_custom_call" | custom-call | tf_op jit(solution)/shard_map/weights/pallas_call | solution.py:27
  69.5 0.0 collective-permute-done.11.refs_4_
  69.5 0.0 collective-permute-done.12.refs_5_
  69.5 0.0 collective-permute-done.10.refs_2_
  69.5 0.0 collective-permute-done.9.refs_1_
  69.5 1.9 %apply.1 = (f32[64,1536]{1,0:T(8,128)S(1)}, f32[64,1536]{1,0:T(8,128)S(1)}, f32[64,1536]{1,0:T(8,128)S(1)}, f32[64,1536]{1,0:T(8,128)S(1)}) custom-call(f32[256,256]{1,0:T(8,128)S(1)} %weights.1, f32[64,1536]{1,0:T(8,128)S(1)} %get-tuple-element.41.refs_0_, f32[64,1536]{1,0:T(8,128)S(1)} %collective-permute-done.9.refs_1_, ...), custom_call_target="tpu_custom_call" | custom-call | tf_op jit(solution)/shard_map/apply/pallas_call | solution.py:27
  71.4 0.1 collective-permute-start.13
  71.5 0.1 collective-permute-start.14
  71.6 2.5 %collective-permute-start.15 = (f32[64,1536]{1,0:T(8,128)S(1)}, f32[64,1536]{1,0:T(8,128)S(1)}, u32[]{:S(2)}, u32[]{:S(2)}) collective-permute-start(f32[64,1536]{1,0:T(8,128)S(1)} %get-tuple-element.54), channel_id=1, source_target_pairs={{24,0},{16,8},{8,16},{0,24},{25,1},{17,9},{9,17},{1,25},{26,2},{18... | collective-permute-start | bytes 1179656 | tf_op jit(solution)/shard_map/ppermute | solution.py:559
  74.1 10.4 %collective-permute-done.13.refs_1_ = f32[64,1536]{1,0:T(8,128)S(1)} collective-permute-done((f32[64,1536]{1,0:T(8,128)S(1)}, f32[64,1536]{1,0:T(8,128)S(1)}, u32[]{:S(2)}, u32[]{:S(2)}) %collective-permute-start.13) | collective-permute-done | bytes 393248 | tf_op jit(solution)/shard_map/ppermute | solution.py:559
  84.6 12.8 %collective-permute-done.14.refs_2_ = f32[64,1536]{1,0:T(8,128)S(1)} collective-permute-done((f32[64,1536]{1,0:T(8,128)S(1)}, f32[64,1536]{1,0:T(8,128)S(1)}, u32[]{:S(2)}, u32[]{:S(2)}) %collective-permute-start.14) | collective-permute-done | bytes 393248 | tf_op jit(solution)/shard_map/ppermute | solution.py:559
  97.3 10.0 %collective-permute-done.15.refs_3_ = f32[64,1536]{1,0:T(8,128)S(1)} collective-permute-done((f32[64,1536]{1,0:T(8,128)S(1)}, f32[64,1536]{1,0:T(8,128)S(1)}, u32[]{:S(2)}, u32[]{:S(2)}) %collective-permute-start.15) | collective-permute-done | bytes 393248 | tf_op jit(solution)/shard_map/ppermute | solution.py:559
  107.3 2.1 %unpack.1 = f32[3,1024,128]{2,1,0:T(8,128)} custom-call(f32[64,1536]{1,0:T(8,128)S(1)} %get-tuple-element.51.refs_0_, f32[64,1536]{1,0:T(8,128)S(1)} %collective-permute-done.13.refs_1_, f32[64,1536]{1,0:T(8,128)S(1)} %collective-permute-done.14.refs_2_, f32[64,1536]{1,0:T(8,128)S(1)} %collective-permute-done.15.refs_3_), custom_call_target="tpu_custom_call" | custom-call | tf_op jit(solution)/shard_map/unpack/pallas_call | solution.py:27
Async XLA Ops:
  0.0 1.4 %copy-start = (f32[3,64,8,256]{3,2,1,0:T(8,128)S(1)}, f32[3,64,8,256]{3,2,1,0:T(8,128)}, u32[]{:S(2)}) copy-start(f32[3,64,8,256]{3,2,1,0:T(8,128)} %param.4) | copy-start | bytes 4718596
  1.4 19.5 %copy-start.3 = (s32[8,4,256]{2,1,0:T(4,128)S(1)}, s32[8,4,256]{2,1,0:T(4,128)}, u32[]{:S(2)}) copy-start(s32[8,4,256]{2,1,0:T(4,128)} %cells.5) | copy-start | bytes 98308
  2.6 23.6 %collective-permute-start.2 = (f32[64,1792]{1,0:T(8,128)S(1)}, f32[64,1792]{1,0:T(8,128)S(1)}, u32[]{:S(2)}, u32[]{:S(2)}) collective-permute-start(f32[64,1792]{1,0:T(8,128)S(1)} %early.1), channel_id=1, source_target_pairs={{0,16},{8,24},{16,0},{24,8},{1,17},{9,25},{17,1},{25,9},{2,18},{10... | collective-permute-start | bytes 1376264 | tf_op jit(solution)/shard_map/ppermute | solution.py:484
  8.4 0.8 copy-start.8
  9.2 12.5 %copy-start.7 = (f32[2,4,64,256]{3,2,1,0:T(8,128)}, f32[2,4,64,256]{3,2,1,0:T(8,128)S(1)}, u32[]{:S(2)}) copy-start(f32[2,4,64,256]{3,2,1,0:T(8,128)S(1)} %get-tuple-element.40) | copy-start | bytes 1572868
  9.2 4.0 %collective-permute-start = (f32[4,64,256]{2,1,0:T(8,128)S(1)}, f32[4,64,256]{2,1,0:T(8,128)S(1)}, u32[]{:S(2)}, u32[]{:S(2)}) collective-permute-start(f32[4,64,256]{2,1,0:T(8,128)S(1)} %get-tuple-element.32), channel_id=1, source_target_pairs={{0,1},{2,3},{4,5},{6,7},{1,0},{3,2},{5,4},{7,6},{8,9},{10,11},{12,... | collective-permute-start | bytes 786440 | tf_op jit(solution)/shard_map/ppermute | solution.py:493
  10.1 10.8 %collective-permute-start.1 = (f32[4,64,256]{2,1,0:T(8,128)S(1)}, f32[4,64,256]{2,1,0:T(8,128)S(1)}, u32[]{:S(2)}, u32[]{:S(2)}) collective-permute-start(f32[4,64,256]{2,1,0:T(8,128)S(1)} %get-tuple-element.33), channel_id=1, source_target_pairs={{1,2},{3,4},{5,6},{2,1},{4,3},{6,5},{9,10},{11,12},{13,14},{10,9},... | collective-permute-start | bytes 786440 | tf_op jit(solution)/shard_map/ppermute | solution.py:492
  21.7 0.7 copy-start.4
  22.4 9.8 %all-to-all-start = ((f32[4,64,256]{2,1,0:T(8,128)}), f32[4,64,256]{2,1,0:T(8,128)S(1)}, u32[]{:S(2)}, u32[]{:S(2)}) async-start(f32[4,64,256]{2,1,0:T(8,128)} %copy-done.4), calls=%async_computation | async-start | bytes 524288 | tf_op jit(solution)/shard_map/all_to_all | solution.py:500
  26.2 0.8 copy-start.1
  27.0 12.6 %collective-permute-start.5 = (f32[2,4,64,256]{3,2,1,0:T(8,128)}, f32[2,4,64,256]{3,2,1,0:T(8,128)S(1)}, u32[]{:S(2)}, u32[]{:S(2)}) collective-permute-start(f32[2,4,64,256]{3,2,1,0:T(8,128)} %copy-done.8), channel_id=1, source_target_pairs={{0,1},{2,3},{4,5},{6,7},{1,0},{3,2},{5,4},{7,6},{8,9},{10,11},{12,... | collective-permute-start | bytes 1572872 | tf_op jit(solution)/shard_map/ppermute | solution.py:502
  27.0 17.0 %collective-permute-start.6 = (f32[2,4,64,256]{3,2,1,0:T(8,128)}, f32[2,4,64,256]{3,2,1,0:T(8,128)S(1)}, u32[]{:S(2)}, u32[]{:S(2)}) collective-permute-start(f32[2,4,64,256]{3,2,1,0:T(8,128)} %copy-done.7), channel_id=1, source_target_pairs={{1,2},{3,4},{5,6},{2,1},{4,3},{6,5},{9,10},{11,12},{13,14},{10,9},... | collective-permute-start | bytes 1572872 | tf_op jit(solution)/shard_map/ppermute | solution.py:501
  32.2 12.7 %collective-permute-start.3 = (f32[256,256]{1,0:T(8,128)S(1)}, f32[256,256]{1,0:T(8,128)S(1)}, u32[]{:S(2)}, u32[]{:S(2)}) collective-permute-start(f32[256,256]{1,0:T(8,128)S(1)} %bitcast.13), channel_id=1, source_target_pairs={{8,16},{16,8},{9,17},{17,9},{10,18},{18,10},{11,19},{19,11},{12,20... | collective-permute-start | bytes 786440 | tf_op jit(solution)/shard_map/ppermute | solution.py:523
  34.1 10.7 %collective-permute-start.4 = (f32[256,256]{1,0:T(8,128)S(1)}, f32[256,256]{1,0:T(8,128)S(1)}, u32[]{:S(2)}, u32[]{:S(2)}) collective-permute-start(f32[256,256]{1,0:T(8,128)S(1)} %bitcast.14), channel_id=1, source_target_pairs={{0,8},{16,24},{8,0},{24,16},{1,9},{17,25},{9,1},{25,17},{2,10},{18... | collective-permute-start | bytes 786440 | tf_op jit(solution)/shard_map/ppermute | solution.py:524
  34.4 1.0 copy-start.2
  44.1 0.8 copy-start.5
  44.1 0.8 copy-start.6
  45.8 8.5 %collective-permute-start.7 = (f32[272,256]{1,0:T(8,128)S(1)}, f32[272,256]{1,0:T(8,128)S(1)}, u32[]{:S(2)}, u32[]{:S(2)}) collective-permute-start(f32[272,256]{1,0:T(8,128)S(1)} %get-tuple-element.47), channel_id=1, source_target_pairs={{0,1},{2,3},{4,5},{6,7},{1,0},{3,2},{5,4},{7,6},{8,9},{10,11},{12,... | collective-permute-start | bytes 835592 | tf_op jit(solution)/shard_map/ppermute | solution.py:536
  45.9 23.6 %collective-permute-start.10 = (f32[64,1536]{1,0:T(8,128)S(1)}, f32[64,1536]{1,0:T(8,128)S(1)}, u32[]{:S(2)}, u32[]{:S(2)}) collective-permute-start(f32[64,1536]{1,0:T(8,128)S(1)} %get-tuple-element.43), channel_id=1, source_target_pairs={{0,24},{8,16},{16,8},{24,0},{1,25},{9,17},{17,9},{25,1},{2,26},{10... | collective-permute-start | bytes 1179656 | tf_op jit(solution)/shard_map/ppermute | solution.py:510
  46.4 23.1 %collective-permute-start.9 = (f32[64,1536]{1,0:T(8,128)S(1)}, f32[64,1536]{1,0:T(8,128)S(1)}, u32[]{:S(2)}, u32[]{:S(2)}) collective-permute-start(f32[64,1536]{1,0:T(8,128)S(1)} %get-tuple-element.42), channel_id=1, source_target_pairs={{0,8},{8,0},{16,24},{24,16},{1,9},{9,1},{17,25},{25,17},{2,10},{10... | collective-permute-start | bytes 1179656 | tf_op jit(solution)/shard_map/ppermute | solution.py:510
  48.7 12.7 %collective-permute-start.8 = (f32[272,256]{1,0:T(8,128)S(1)}, f32[272,256]{1,0:T(8,128)S(1)}, u32[]{:S(2)}, u32[]{:S(2)}) collective-permute-start(f32[272,256]{1,0:T(8,128)S(1)} %get-tuple-element.48), channel_id=1, source_target_pairs={{1,2},{3,4},{5,6},{2,1},{4,3},{6,5},{9,10},{11,12},{13,14},{10,9},... | collective-permute-start | bytes 835592 | tf_op jit(solution)/shard_map/ppermute | solution.py:535
  54.3 15.2 %collective-permute-start.11 = (f32[64,768]{1,0:T(8,128)S(1)}, f32[64,768]{1,0:T(8,128)S(1)}, u32[]{:S(2)}, u32[]{:S(2)}) collective-permute-start(f32[64,768]{1,0:T(8,128)S(1)} %get-tuple-element.49), channel_id=1, source_target_pairs={{0,1},{2,3},{4,5},{6,7},{1,0},{3,2},{5,4},{7,6},{8,9},{10,11},{12,... | collective-permute-start | bytes 589832 | tf_op jit(solution)/shard_map/ppermute | solution.py:521
  54.4 15.1 %collective-permute-start.12 = (f32[64,768]{1,0:T(8,128)S(1)}, f32[64,768]{1,0:T(8,128)S(1)}, u32[]{:S(2)}, u32[]{:S(2)}) collective-permute-start(f32[64,768]{1,0:T(8,128)S(1)} %get-tuple-element.50), channel_id=1, source_target_pairs={{1,2},{3,4},{5,6},{2,1},{4,3},{6,5},{9,10},{11,12},{13,14},{10,9},... | collective-permute-start | bytes 589832 | tf_op jit(solution)/shard_map/ppermute | solution.py:520
  71.4 13.1 %collective-permute-start.13 = (f32[64,1536]{1,0:T(8,128)S(1)}, f32[64,1536]{1,0:T(8,128)S(1)}, u32[]{:S(2)}, u32[]{:S(2)}) collective-permute-start(f32[64,1536]{1,0:T(8,128)S(1)} %get-tuple-element.52), channel_id=1, source_target_pairs={{8,0},{0,8},{24,16},{16,24},{9,1},{1,9},{25,17},{17,25},{10,2},{2,... | collective-permute-start | bytes 1179656 | tf_op jit(solution)/shard_map/ppermute | solution.py:559
  71.5 25.8 %collective-permute-start.14 = (f32[64,1536]{1,0:T(8,128)S(1)}, f32[64,1536]{1,0:T(8,128)S(1)}, u32[]{:S(2)}, u32[]{:S(2)}) collective-permute-start(f32[64,1536]{1,0:T(8,128)S(1)} %get-tuple-element.53), channel_id=1, source_target_pairs={{16,0},{24,8},{0,16},{8,24},{17,1},{25,9},{1,17},{9,25},{18,2},{26... | collective-permute-start | bytes 1179656 | tf_op jit(solution)/shard_map/ppermute | solution.py:559
  71.6 35.7 %collective-permute-start.15 = (f32[64,1536]{1,0:T(8,128)S(1)}, f32[64,1536]{1,0:T(8,128)S(1)}, u32[]{:S(2)}, u32[]{:S(2)}) collective-permute-start(f32[64,1536]{1,0:T(8,128)S(1)} %get-tuple-element.54), channel_id=1, source_target_pairs={{24,0},{16,8},{8,16},{0,24},{25,1},{17,9},{9,17},{1,25},{26,2},{18... | collective-permute-start | bytes 1179656 | tf_op jit(solution)/shard_map/ppermute | solution.py:559

commit v2 on v1

--- a/solution.py
+++ b/solution.py
@@ -21,14 +21,14 @@
 BF16 = jnp.bfloat16
 
 
-def call(kernel, outs, *args, name, flops=0, limit=LIMIT):
+def call(kernel, outs, *args, name, flops=0, limit=LIMIT, far_out=False):
     shapes = [jax.ShapeDtypeStruct(s, F32) for s in outs[0]]
     bytes_moved = 0
     return pl.pallas_call(
         kernel,
         out_shape=shapes,
         in_specs=[pl.BlockSpec(memory_space=pltpu.VMEM)] * len(args),
-        out_specs=[pl.BlockSpec(memory_space=pltpu.VMEM)] * len(shapes),
+        out_specs=[pl.BlockSpec(memory_space=pl.ANY if far_out else pltpu.VMEM)] * len(shapes),
         scratch_shapes=outs[1],
         compiler_params=pltpu.CompilerParams(vmem_limit_bytes=limit * 2**20),
         cost_estimate=pl.CostEstimate(flops=0, bytes_accessed=bytes_moved, transcendentals=0),
@@ -45,7 +45,9 @@
     ah, al = a
     bh, bl = b
     dot = functools.partial(lax.dot_general, dimension_numbers=dims, preferred_element_type=F32)
-    return dot(ah, bh) + (dot(ah, bl) + dot(al, bh))
+    rows = ah.shape[0]
+    both = dot(jnp.concatenate([ah, al], axis=0), bh)
+    return both[:rows] + (both[rows:] + dot(ah, bl))
 
 
 def coefficients(rows):
@@ -150,7 +152,7 @@
                     uv_cross[f, i, at, cols] = jnp.where(even, up[f + 1][t], down[f + 1][t])
         return 0
 
-    lax.fori_loop(0, members // 8, block, 0)
+    lax.fori_loop(0, members // 8, block, 0, unroll=2)
 
 
 def early_kernel(width, n, shift, rows, state, out):
@@ -245,7 +247,7 @@
                 to_cross[at, cols] = jnp.where(even, up, down)
         return 0
 
-    lax.fori_loop(0, members // 8, block, 0)
+    lax.fori_loop(0, members // 8, block, 0, unroll=2)
 
 
 def halo_places(rows):
@@ -430,8 +432,9 @@
 
 
 def unpack_kernel(width, n, rows, *refs):
-    *parts, out, whole = refs
+    *parts, out, whole, done, sems = refs
     members = parts[0].shape[0]
+    copies = []
     mine = lax.axis_index("member")
     for s, part in enumerate(parts):
         whole[owner_of(mine, s, n)] = part[...]
@@ -450,7 +453,11 @@
                         if i != j:
                             line = pltpu.roll(line, (i - j) * width % LANES, 1)
                         total = line if total is None else jnp.where(slot == i, line, total)
-                    out[f, pl.ds(t * rows + r + j, members, stride=rows * tiles), :] = total
+                    done[f, pl.ds(t * rows + r + j, members, stride=rows * tiles), :] = total
+        copies.append(pltpu.make_async_copy(done.at[f], out.at[f], sems.at[f]))
+        copies[-1].start()
+    for copy in copies:
+        copy.wait()
 
 
 def after(array, *others):
@@ -534,6 +541,7 @@
     )
     gram_cross = lax.ppermute(gram_cross, "lat", cross_lat)
     gram_pair = lax.ppermute(gram_pair, "lat", pair_lat)
+    raw_cross, raw_pair = lax.optimization_barrier((raw_cross, raw_pair, early_cross, early_pair))[:2]
     (gram_own,) = call(
         functools.partial(gram_kernel, (0,), *sizes),
         ([gram_shape], []),
@@ -559,9 +567,17 @@
         final[s] = lax.ppermute(done[s], "member", back)
     (analysis,) = call(
         functools.partial(unpack_kernel, width, n_member, rows),
-        ([(3, members * tiles * rows, LANES)], [pltpu.VMEM((n_member,) + shape, F32)]),
+        (
+            [(3, members * tiles * rows, LANES)],
+            [
+                pltpu.VMEM((n_member,) + shape, F32),
+                pltpu.VMEM((3, members * tiles * rows, LANES), F32),
+                pltpu.SemaphoreType.DMA((3,)),
+            ],
+        ),
         *final,
         name="unpack",
+        far_out=True,
     )
     analysis = analysis.reshape(3, members, tiles, rows, LANES).transpose(0, 1, 3, 2, 4)
     return analysis.reshape(ensemble_state.shape)

time: 110 us -> 108 us (0.982)
  waiting for transfers between devices: 51.3 us -> 47.4 us
  starting transfers between devices: 29.2 us -> 32.6 us
  Pallas kernels: 23.9 us -> 21.7 us
    ppermute x1, waiting for transfers between devices: 4.41 us -> 0.52 us  [body(): uv_cross = lax.ppermute(after(uv_cross, early_block), 'lat', cross_lat)]
    pallas_call x10, Pallas kernels: 23.9 us -> 21.7 us  [call(): pl.pallas_call(kernel, out_shape=shapes, in_specs=[pl.BlockSpec(memory_sp...]
    ppermute x1, starting transfers between devices: 2.26 us -> 3.62 us  [body(): early_cross = lax.ppermute(early_cross, 'lat', cross_lat)]
    ppermute x1, waiting for transfers between devices: 0.01 us -> 1.33 us  [body(): early_pair = lax.ppermute(early_pair, 'lat', pair_lat)]
  transfers between devices with their start and end apart: 17 -> 17, of which waited for: 7 -> 8; matrix products, arithmetic and copies ran while one was open for 0% -> 0% of each run, Pallas kernels for 16% -> 16%
where the time goes in v2:
time: 108 us; the launch traced here: 107 us
  waiting for transfers between devices  47.4 us (44%)
  starting transfers between devices  32.6 us (30%)
  Pallas kernels  21.7 us (20%)
  local copies, waits for them, and re-layouts  4.72 us (4%)
    ppermute x3, waiting for transfers between devices, body(): final[s] = lax.ppermute(done[s], 'member', back)  32.9 us
    pallas_call x10, Pallas kernels, call(): pl.pallas_call(kernel, out_shape=shapes, in_specs=[pl.BlockSpec(memory_sp...  21.7 us
    ppermute x1, waiting for transfers between devices, body(): got_cross = lax.ppermute(h_cross, 'lat', cross_lat)  7.74 us
    ppermute x1, starting transfers between devices, body(): gram_cross = lax.ppermute(gram_cross, 'lat', cross_lat)  5.92 us
    unnamed x18, local copies, waits for them, and re-layouts  4.72 us
    ppermute x1, starting transfers between devices, body(): uv_cross = lax.ppermute(after(uv_cross, early_block), 'lat', cross_lat)  3.9 us
    all_to_all x1, starting transfers between devices, body(): lax.all_to_all(seen, 'member', split_axis=0, concat_axis=0, tiled=True)  3.82 us
    ppermute x1, waiting for transfers between devices, body(): gram_cross = lax.ppermute(gram_cross, 'lat', cross_lat)  3.66 us
  transfers between devices with their start and end apart: 17, of which 8 were waited for; matrix products, arithmetic and copies ran while one was open for 0% of the time, Pallas kernels for 16%

profile of v2, /device:TPU:11, one launch (start us, length us, event | category | flops | bytes accessed | tf_op | source)
XLA Modules:
  0.0 106.9 jit_solution(4675134997973091984)
XLA Ops:
  0.0 0.0 copy-start
  0.0 1.4 %copy-done = f32[3,64,8,256]{3,2,1,0:T(8,128)S(1)} copy-done((f32[3,64,8,256]{3,2,1,0:T(8,128)S(1)}, f32[3,64,8,256]{3,2,1,0:T(8,128)}, u32[]{:S(2)}) %copy-start) | copy-done | bytes 1572888
  1.4 0.0 copy-start.3
  1.4 1.2 %early.1 = f32[64,1792]{1,0:T(8,128)S(1)} custom-call(f32[3,1024,128]{2,1,0:T(8,128)S(1)} %bitcast.11), custom_call_target="tpu_custom_call" | custom-call | tf_op jit(solution)/shard_map/early/pallas_call | solution.py:27
  2.6 2.3 %collective-permute-start.2 = (f32[64,1792]{1,0:T(8,128)S(1)}, f32[64,1792]{1,0:T(8,128)S(1)}, u32[]{:S(2)}, u32[]{:S(2)}) collective-permute-start(f32[64,1792]{1,0:T(8,128)S(1)} %early.1), channel_id=1, source_target_pairs={{0,16},{8,24},{16,0},{24,8},{1,17},{9,25},{17,1},{25,9},{2,18},{10... | collective-permute-start | bytes 1376264 | tf_op jit(solution)/shard_map/ppermute | solution.py:491
  4.9 3.1 %model.1 = (f32[3,8,64,256]{3,2,1,0:T(8,128)S(1)}, f32[4,64,256]{2,1,0:T(8,128)S(1)}, f32[4,64,256]{2,1,0:T(8,128)S(1)}, f32[2,4,64,256]{3,2,1,0:T(8,128)S(1)}, f32[2,4,64,256]{3,2,1,0:T(8,128)S(1)}) custom-call(f32[3,1024,128]{2,1,0:T(8,128)S(1)} %bitcast.12), custom_call_target="tpu_custom_call" | custom-call | tf_op jit(solution)/shard_map/model/pallas_call | solution.py:27
  8.1 0.0 copy-start.8
  8.1 0.8 copy-done.8
  8.9 0.0 copy-start.7
  8.9 1.0 collective-permute-start
  9.8 3.0 %collective-permute-start.1 = (f32[4,64,256]{2,1,0:T(8,128)S(1)}, f32[4,64,256]{2,1,0:T(8,128)S(1)}, u32[]{:S(2)}, u32[]{:S(2)}) collective-permute-start(f32[4,64,256]{2,1,0:T(8,128)S(1)} %get-tuple-element.35), channel_id=1, source_target_pairs={{1,2},{3,4},{5,6},{2,1},{4,3},{6,5},{9,10},{11,12},{13,14},{10,9},... | collective-permute-start | bytes 786440 | tf_op jit(solution)/shard_map/ppermute | solution.py:499
  12.8 0.0 collective-permute-done.got_pair
  12.8 7.7 %collective-permute-done.1.got_cross = f32[4,64,256]{2,1,0:T(8,128)S(1)} collective-permute-done((f32[4,64,256]{2,1,0:T(8,128)S(1)}, f32[4,64,256]{2,1,0:T(8,128)S(1)}, u32[]{:S(2)}, u32[]{:S(2)}) %collective-permute-start.1) | collective-permute-done | bytes 262176 | tf_op jit(solution)/shard_map/ppermute | solution.py:499
  20.6 0.0 copy-done.3
  20.6 0.8 observe.1
  21.4 0.0 copy-done.7
  21.4 0.0 copy-start.4
  21.4 0.7 copy-done.4
  22.1 3.8 %all-to-all-start = ((f32[4,64,256]{2,1,0:T(8,128)}), f32[4,64,256]{2,1,0:T(8,128)S(1)}, u32[]{:S(2)}, u32[]{:S(2)}) async-start(f32[4,64,256]{2,1,0:T(8,128)} %copy-done.4), calls=%async_computation | async-start | bytes 524288 | tf_op jit(solution)/shard_map/all_to_all | solution.py:507
  25.9 0.0 collective-permute-done.2.block_in
  25.9 0.0 copy-start.1
  25.9 0.8 copy-done.1
  26.7 0.0 collective-permute-start.5
  26.7 3.9 %collective-permute-start.6 = (f32[2,4,64,256]{3,2,1,0:T(8,128)}, f32[2,4,64,256]{3,2,1,0:T(8,128)S(1)}, u32[]{:S(2)}, u32[]{:S(2)}) collective-permute-start(f32[2,4,64,256]{3,2,1,0:T(8,128)} %copy-done.7), channel_id=1, source_target_pairs={{1,2},{3,4},{5,6},{2,1},{4,3},{6,5},{9,10},{11,12},{13,14},{10,9},... | collective-permute-start | bytes 1572872 | tf_op jit(solution)/shard_map/ppermute | solution.py:508
  30.6 1.3 %all-to-all-done = f32[4,64,256]{2,1,0:T(8,128)S(1)} async-done(((f32[4,64,256]{2,1,0:T(8,128)}), f32[4,64,256]{2,1,0:T(8,128)S(1)}, u32[]{:S(2)}, u32[]{:S(2)}) %all-to-all-start) | async-done | bytes 262176 | tf_op jit(solution)/shard_map/all_to_all | solution.py:507
  31.9 2.0 %collective-permute-start.3 = (f32[256,256]{1,0:T(8,128)S(1)}, f32[256,256]{1,0:T(8,128)S(1)}, u32[]{:S(2)}, u32[]{:S(2)}) collective-permute-start(f32[256,256]{1,0:T(8,128)S(1)} %bitcast.13), channel_id=1, source_target_pairs={{8,16},{16,8},{9,17},{17,9},{10,18},{18,10},{11,19},{19,11},{12,20... | collective-permute-start | bytes 786440 | tf_op jit(solution)/shard_map/ppermute | solution.py:530
  33.8 0.3 collective-permute-start.4
  34.1 0.0 copy-start.2
  34.1 1.0 copy-done.2
  35.2 3.3 %owner_model.1 = (f32[64,1536]{1,0:T(8,128)S(1)}, f32[64,768]{1,0:T(8,128)S(1)}, f32[64,768]{1,0:T(8,128)S(1)}) custom-call(f32[64,1792]{1,0:T(8,128)S(1)} %copy-done.2), custom_call_target="tpu_custom_call" | custom-call | tf_op jit(solution)/shard_map/owner_model/pallas_call | solution.py:27
  38.5 3.6 %collective-permute-start.7 = (f32[64,768]{1,0:T(8,128)S(1)}, f32[64,768]{1,0:T(8,128)S(1)}, u32[]{:S(2)}, u32[]{:S(2)}) collective-permute-start(f32[64,768]{1,0:T(8,128)S(1)} %get-tuple-element.49), channel_id=1, source_target_pairs={{1,2},{3,4},{5,6},{2,1},{4,3},{6,5},{9,10},{11,12},{13,14},{10,9},... | collective-permute-start | bytes 589832 | tf_op jit(solution)/shard_map/ppermute | solution.py:527
  42.1 0.0 collective-permute-done.5.got_pair
  42.1 0.5 collective-permute-done.6.got_cross
  42.7 0.0 copy-start.5
  42.7 0.0 copy-start.6
  42.7 0.8 pack.1
  43.4 1.3 %collective-permute-start.11 = (f32[64,1536]{1,0:T(8,128)S(1)}, f32[64,1536]{1,0:T(8,128)S(1)}, u32[]{:S(2)}, u32[]{:S(2)}) collective-permute-start(f32[64,1536]{1,0:T(8,128)S(1)} %get-tuple-element.44), channel_id=1, source_target_pairs={{0,8},{8,0},{16,24},{24,16},{1,9},{9,1},{17,25},{25,17},{2,10},{10... | collective-permute-start | bytes 1179656 | tf_op jit(solution)/shard_map/ppermute | solution.py:517
  44.8 2.2 %collective-permute-start.12 = (f32[64,1536]{1,0:T(8,128)S(1)}, f32[64,1536]{1,0:T(8,128)S(1)}, u32[]{:S(2)}, u32[]{:S(2)}) collective-permute-start(f32[64,1536]{1,0:T(8,128)S(1)} %get-tuple-element.45), channel_id=1, source_target_pairs={{0,24},{8,16},{16,8},{24,0},{1,25},{9,17},{17,9},{25,1},{2,26},{10... | collective-permute-start | bytes 1179656 | tf_op jit(solution)/shard_map/ppermute | solution.py:517
  47.0 0.0 collective-permute-done.3.raw_cross
  47.0 0.0 collective-permute-done.4.raw_pair
  47.0 0.0 copy-done.5
  47.0 0.0 copy-done.6
  47.0 0.9 gram_beside.1
  47.9 5.9 %collective-permute-start.10 = (f32[272,256]{1,0:T(8,128)S(1)}, f32[272,256]{1,0:T(8,128)S(1)}, u32[]{:S(2)}, u32[]{:S(2)}) collective-permute-start(f32[272,256]{1,0:T(8,128)S(1)} %get-tuple-element.54), channel_id=1, source_target_pairs={{1,2},{3,4},{5,6},{2,1},{4,3},{6,5},{9,10},{11,12},{13,14},{10,9},... | collective-permute-start | bytes 835592 | tf_op jit(solution)/shard_map/ppermute | solution.py:542
  53.8 0.1 collective-permute-start.9
  53.9 0.0 collective-permute-done.7.refs_5_
  53.9 0.5 collective-permute-start.8
  54.4 1.3 %collective-permute-done.8.refs_4_ = f32[64,768]{1,0:T(8,128)S(1)} collective-permute-done((f32[64,768]{1,0:T(8,128)S(1)}, f32[64,768]{1,0:T(8,128)S(1)}, u32[]{:S(2)}, u32[]{:S(2)}) %collective-permute-start.8) | collective-permute-done | bytes 196640 | tf_op jit(solution)/shard_map/ppermute | solution.py:528
  55.7 0.6 gram_own.1.own
  56.3 3.7 %collective-permute-done.10.got_cross = f32[272,256]{1,0:T(8,128)S(1)} collective-permute-done((f32[272,256]{1,0:T(8,128)S(1)}, f32[272,256]{1,0:T(8,128)S(1)}, u32[]{:S(2)}, u32[]{:S(2)}) %collective-permute-start.10) | collective-permute-done | bytes 278560 | tf_op jit(solution)/shard_map/ppermute | solution.py:542
  60.0 0.0 collective-permute-done.9.got_pair
  60.0 8.0 %weights.1 = f32[256,256]{1,0:T(8,128)S(1)} custom-call(f32[272,256]{1,0:T(8,128)S(1)} %gram_own.1.own, f32[272,256]{1,0:T(8,128)S(1)} %collective-permute-done.9.got_pair, f32[272,256]{1,0:T(8,128)S(1)} %collective-permute-done.10.got_cross), custom_call_target="tpu_custom_call" | custom-call | tf_op jit(solution)/shard_map/weights/pallas_call | solution.py:27
  68.0 0.0 collective-permute-done.11.refs_1_
  68.0 0.0 collective-permute-done.12.refs_2_
  68.0 1.3 %apply.1 = (f32[64,1536]{1,0:T(8,128)S(1)}, f32[64,1536]{1,0:T(8,128)S(1)}, f32[64,1536]{1,0:T(8,128)S(1)}, f32[64,1536]{1,0:T(8,128)S(1)}) custom-call(f32[256,256]{1,0:T(8,128)S(1)} %weights.1, f32[64,1536]{1,0:T(8,128)S(1)} %get-tuple-element.43.refs_0_, f32[64,1536]{1,0:T(8,128)S(1)} %collective-permute-done.11.refs_1_, ...), custom_call_target="tpu_custom_call" | custom-call | tf_op jit(solution)/shard_map/apply/pallas_call | solution.py:27
  69.3 1.1 collective-permute-start.13
  70.4 0.1 collective-permute-start.14
  70.4 1.6 %collective-permute-start.15 = (f32[64,1536]{1,0:T(8,128)S(1)}, f32[64,1536]{1,0:T(8,128)S(1)}, u32[]{:S(2)}, u32[]{:S(2)}) collective-permute-start(f32[64,1536]{1,0:T(8,128)S(1)} %get-tuple-element.58), channel_id=1, source_target_pairs={{24,0},{16,8},{8,16},{0,24},{25,1},{17,9},{9,17},{1,25},{26,2},{18... | collective-permute-start | bytes 1179656 | tf_op jit(solution)/shard_map/ppermute | solution.py:567
  72.0 12.6 %collective-permute-done.13.refs_1_ = f32[64,1536]{1,0:T(8,128)S(1)} collective-permute-done((f32[64,1536]{1,0:T(8,128)S(1)}, f32[64,1536]{1,0:T(8,128)S(1)}, u32[]{:S(2)}, u32[]{:S(2)}) %collective-permute-start.13) | collective-permute-done | bytes 393248 | tf_op jit(solution)/shard_map/ppermute | solution.py:567
  84.7 11.6 %collective-permute-done.14.refs_2_ = f32[64,1536]{1,0:T(8,128)S(1)} collective-permute-done((f32[64,1536]{1,0:T(8,128)S(1)}, f32[64,1536]{1,0:T(8,128)S(1)}, u32[]{:S(2)}, u32[]{:S(2)}) %collective-permute-start.14) | collective-permute-done | bytes 393248 | tf_op jit(solution)/shard_map/ppermute | solution.py:567
  96.3 8.7 %collective-permute-done.15.refs_3_ = f32[64,1536]{1,0:T(8,128)S(1)} collective-permute-done((f32[64,1536]{1,0:T(8,128)S(1)}, f32[64,1536]{1,0:T(8,128)S(1)}, u32[]{:S(2)}, u32[]{:S(2)}) %collective-permute-start.15) | collective-permute-done | bytes 393248 | tf_op jit(solution)/shard_map/ppermute | solution.py:567
  104.9 1.8 %unpack.1 = f32[3,1024,128]{2,1,0:T(8,128)} custom-call(f32[64,1536]{1,0:T(8,128)S(1)} %get-tuple-element.55.refs_0_, f32[64,1536]{1,0:T(8,128)S(1)} %collective-permute-done.13.refs_1_, f32[64,1536]{1,0:T(8,128)S(1)} %collective-permute-done.14.refs_2_, f32[64,1536]{1,0:T(8,128)S(1)} %collective-permute-done.15.refs_3_), custom_call_target="tpu_custom_call" | custom-call | tf_op jit(solution)/shard_map/unpack/pallas_call | solution.py:27
Async XLA Ops:
  0.0 1.4 %copy-start = (f32[3,64,8,256]{3,2,1,0:T(8,128)S(1)}, f32[3,64,8,256]{3,2,1,0:T(8,128)}, u32[]{:S(2)}) copy-start(f32[3,64,8,256]{3,2,1,0:T(8,128)} %param.4) | copy-start | bytes 4718596
  1.4 19.2 %copy-start.3 = (s32[8,4,256]{2,1,0:T(4,128)S(1)}, s32[8,4,256]{2,1,0:T(4,128)}, u32[]{:S(2)}) copy-start(s32[8,4,256]{2,1,0:T(4,128)} %cells.5) | copy-start | bytes 98308
  2.6 23.3 %collective-permute-start.2 = (f32[64,1792]{1,0:T(8,128)S(1)}, f32[64,1792]{1,0:T(8,128)S(1)}, u32[]{:S(2)}, u32[]{:S(2)}) collective-permute-start(f32[64,1792]{1,0:T(8,128)S(1)} %early.1), channel_id=1, source_target_pairs={{0,16},{8,24},{16,0},{24,8},{1,17},{9,25},{17,1},{25,9},{2,18},{10... | collective-permute-start | bytes 1376264 | tf_op jit(solution)/shard_map/ppermute | solution.py:491
  8.1 0.8 copy-start.8
  8.9 12.5 %copy-start.7 = (f32[2,4,64,256]{3,2,1,0:T(8,128)}, f32[2,4,64,256]{3,2,1,0:T(8,128)S(1)}, u32[]{:S(2)}) copy-start(f32[2,4,64,256]{3,2,1,0:T(8,128)S(1)} %get-tuple-element.42) | copy-start | bytes 1572868
  8.9 4.0 %collective-permute-start = (f32[4,64,256]{2,1,0:T(8,128)S(1)}, f32[4,64,256]{2,1,0:T(8,128)S(1)}, u32[]{:S(2)}, u32[]{:S(2)}) collective-permute-start(f32[4,64,256]{2,1,0:T(8,128)S(1)} %get-tuple-element.34), channel_id=1, source_target_pairs={{0,1},{2,3},{4,5},{6,7},{1,0},{3,2},{5,4},{7,6},{8,9},{10,11},{12,... | collective-permute-start | bytes 786440 | tf_op jit(solution)/shard_map/ppermute | solution.py:500
  9.8 10.8 %collective-permute-start.1 = (f32[4,64,256]{2,1,0:T(8,128)S(1)}, f32[4,64,256]{2,1,0:T(8,128)S(1)}, u32[]{:S(2)}, u32[]{:S(2)}) collective-permute-start(f32[4,64,256]{2,1,0:T(8,128)S(1)} %get-tuple-element.35), channel_id=1, source_target_pairs={{1,2},{3,4},{5,6},{2,1},{4,3},{6,5},{9,10},{11,12},{13,14},{10,9},... | collective-permute-start | bytes 786440 | tf_op jit(solution)/shard_map/ppermute | solution.py:499
  21.4 0.7 copy-start.4
  22.1 9.8 %all-to-all-start = ((f32[4,64,256]{2,1,0:T(8,128)}), f32[4,64,256]{2,1,0:T(8,128)S(1)}, u32[]{:S(2)}, u32[]{:S(2)}) async-start(f32[4,64,256]{2,1,0:T(8,128)} %copy-done.4), calls=%async_computation | async-start | bytes 524288 | tf_op jit(solution)/shard_map/all_to_all | solution.py:507
  25.9 0.8 copy-start.1
  26.7 15.4 %collective-permute-start.5 = (f32[2,4,64,256]{3,2,1,0:T(8,128)}, f32[2,4,64,256]{3,2,1,0:T(8,128)S(1)}, u32[]{:S(2)}, u32[]{:S(2)}) collective-permute-start(f32[2,4,64,256]{3,2,1,0:T(8,128)} %copy-done.8), channel_id=1, source_target_pairs={{0,1},{2,3},{4,5},{6,7},{1,0},{3,2},{5,4},{7,6},{8,9},{10,11},{12,... | collective-permute-start | bytes 1572872 | tf_op jit(solution)/shard_map/ppermute | solution.py:509
  26.7 15.9 %collective-permute-start.6 = (f32[2,4,64,256]{3,2,1,0:T(8,128)}, f32[2,4,64,256]{3,2,1,0:T(8,128)S(1)}, u32[]{:S(2)}, u32[]{:S(2)}) collective-permute-start(f32[2,4,64,256]{3,2,1,0:T(8,128)} %copy-done.7), channel_id=1, source_target_pairs={{1,2},{3,4},{5,6},{2,1},{4,3},{6,5},{9,10},{11,12},{13,14},{10,9},... | collective-permute-start | bytes 1572872 | tf_op jit(solution)/shard_map/ppermute | solution.py:508
  31.9 15.1 %collective-permute-start.3 = (f32[256,256]{1,0:T(8,128)S(1)}, f32[256,256]{1,0:T(8,128)S(1)}, u32[]{:S(2)}, u32[]{:S(2)}) collective-permute-start(f32[256,256]{1,0:T(8,128)S(1)} %bitcast.13), channel_id=1, source_target_pairs={{8,16},{16,8},{9,17},{17,9},{10,18},{18,10},{11,19},{19,11},{12,20... | collective-permute-start | bytes 786440 | tf_op jit(solution)/shard_map/ppermute | solution.py:530
  33.8 13.1 %collective-permute-start.4 = (f32[256,256]{1,0:T(8,128)S(1)}, f32[256,256]{1,0:T(8,128)S(1)}, u32[]{:S(2)}, u32[]{:S(2)}) collective-permute-start(f32[256,256]{1,0:T(8,128)S(1)} %bitcast.14), channel_id=1, source_target_pairs={{0,8},{16,24},{8,0},{24,16},{1,9},{17,25},{9,1},{25,17},{2,10},{18... | collective-permute-start | bytes 786440 | tf_op jit(solution)/shard_map/ppermute | solution.py:531
  34.1 1.0 copy-start.2
  38.5 15.4 %collective-permute-start.7 = (f32[64,768]{1,0:T(8,128)S(1)}, f32[64,768]{1,0:T(8,128)S(1)}, u32[]{:S(2)}, u32[]{:S(2)}) collective-permute-start(f32[64,768]{1,0:T(8,128)S(1)} %get-tuple-element.49), channel_id=1, source_target_pairs={{1,2},{3,4},{5,6},{2,1},{4,3},{6,5},{9,10},{11,12},{13,14},{10,9},... | collective-permute-start | bytes 589832 | tf_op jit(solution)/shard_map/ppermute | solution.py:527
  42.7 4.3 %copy-start.5 = (f32[8,4,256]{2,1,0:T(4,128)S(1)}, f32[8,4,256]{2,1,0:T(4,128)}, u32[]{:S(2)}) copy-start(f32[8,4,256]{2,1,0:T(4,128)} %values.3) | copy-start | bytes 98308
  42.7 4.3 %copy-start.6 = (f32[8,4,256]{2,1,0:T(4,128)S(1)}, f32[8,4,256]{2,1,0:T(4,128)}, u32[]{:S(2)}) copy-start(f32[8,4,256]{2,1,0:T(4,128)} %precs.3) | copy-start | bytes 98308
  43.4 24.5 %collective-permute-start.11 = (f32[64,1536]{1,0:T(8,128)S(1)}, f32[64,1536]{1,0:T(8,128)S(1)}, u32[]{:S(2)}, u32[]{:S(2)}) collective-permute-start(f32[64,1536]{1,0:T(8,128)S(1)} %get-tuple-element.44), channel_id=1, source_target_pairs={{0,8},{8,0},{16,24},{24,16},{1,9},{9,1},{17,25},{25,17},{2,10},{10... | collective-permute-start | bytes 1179656 | tf_op jit(solution)/shard_map/ppermute | solution.py:517
  44.8 23.2 %collective-permute-start.12 = (f32[64,1536]{1,0:T(8,128)S(1)}, f32[64,1536]{1,0:T(8,128)S(1)}, u32[]{:S(2)}, u32[]{:S(2)}) collective-permute-start(f32[64,1536]{1,0:T(8,128)S(1)} %get-tuple-element.45), channel_id=1, source_target_pairs={{0,24},{8,16},{16,8},{24,0},{1,25},{9,17},{17,9},{25,1},{2,26},{10... | collective-permute-start | bytes 1179656 | tf_op jit(solution)/shard_map/ppermute | solution.py:517
  47.9 12.1 %collective-permute-start.10 = (f32[272,256]{1,0:T(8,128)S(1)}, f32[272,256]{1,0:T(8,128)S(1)}, u32[]{:S(2)}, u32[]{:S(2)}) collective-permute-start(f32[272,256]{1,0:T(8,128)S(1)} %get-tuple-element.54), channel_id=1, source_target_pairs={{1,2},{3,4},{5,6},{2,1},{4,3},{6,5},{9,10},{11,12},{13,14},{10,9},... | collective-permute-start | bytes 835592 | tf_op jit(solution)/shard_map/ppermute | solution.py:542
  53.8 6.2 %collective-permute-start.9 = (f32[272,256]{1,0:T(8,128)S(1)}, f32[272,256]{1,0:T(8,128)S(1)}, u32[]{:S(2)}, u32[]{:S(2)}) collective-permute-start(f32[272,256]{1,0:T(8,128)S(1)} %get-tuple-element.53), channel_id=1, source_target_pairs={{0,1},{2,3},{4,5},{6,7},{1,0},{3,2},{5,4},{7,6},{8,9},{10,11},{12,... | collective-permute-start | bytes 835592 | tf_op jit(solution)/shard_map/ppermute | solution.py:543
  53.9 1.8 %collective-permute-start.8 = (f32[64,768]{1,0:T(8,128)S(1)}, f32[64,768]{1,0:T(8,128)S(1)}, u32[]{:S(2)}, u32[]{:S(2)}) collective-permute-start(f32[64,768]{1,0:T(8,128)S(1)} %get-tuple-element.50), channel_id=1, source_target_pairs={{0,1},{2,3},{4,5},{6,7},{1,0},{3,2},{5,4},{7,6},{8,9},{10,11},{12,... | collective-permute-start | bytes 589832 | tf_op jit(solution)/shard_map/ppermute | solution.py:528
  69.3 15.4 %collective-permute-start.13 = (f32[64,1536]{1,0:T(8,128)S(1)}, f32[64,1536]{1,0:T(8,128)S(1)}, u32[]{:S(2)}, u32[]{:S(2)}) collective-permute-start(f32[64,1536]{1,0:T(8,128)S(1)} %get-tuple-element.56), channel_id=1, source_target_pairs={{8,0},{0,8},{24,16},{16,24},{9,1},{1,9},{25,17},{17,25},{10,2},{2,... | collective-permute-start | bytes 1179656 | tf_op jit(solution)/shard_map/ppermute | solution.py:567
  70.4 25.9 %collective-permute-start.14 = (f32[64,1536]{1,0:T(8,128)S(1)}, f32[64,1536]{1,0:T(8,128)S(1)}, u32[]{:S(2)}, u32[]{:S(2)}) collective-permute-start(f32[64,1536]{1,0:T(8,128)S(1)} %get-tuple-element.57), channel_id=1, source_target_pairs={{16,0},{24,8},{0,16},{8,24},{17,1},{25,9},{1,17},{9,25},{18,2},{26... | collective-permute-start | bytes 1179656 | tf_op jit(solution)/shard_map/ppermute | solution.py:567
  70.4 34.5 %collective-permute-start.15 = (f32[64,1536]{1,0:T(8,128)S(1)}, f32[64,1536]{1,0:T(8,128)S(1)}, u32[]{:S(2)}, u32[]{:S(2)}) collective-permute-start(f32[64,1536]{1,0:T(8,128)S(1)} %get-tuple-element.58), channel_id=1, source_target_pairs={{24,0},{16,8},{8,16},{0,24},{25,1},{17,9},{9,17},{1,25},{26,2},{18... | collective-permute-start | bytes 1179656 | tf_op jit(solution)/shard_map/ppermute | solution.py:567

commit v3 on v2

--- a/solution.py
+++ b/solution.py
@@ -286,14 +286,8 @@
             seen[q, :, pl.ds(c, LANES)] = total
 
 
-def pack_kernel(width, n, shifts, own, height, got_pair, got_cross, *refs):
-    *outs, wind = refs
-    _, rows, members, lon = own.shape
-    pair, cross = halo_places(rows)
-    wind[...] = own[1:3]
-    for f in range(2):
-        wind[f, pl.ds(pair, HALO)] += got_pair[f]
-        wind[f, pl.ds(cross, HALO)] += got_cross[f]
+def owner_blocks(width, n, shifts, fields, outs):
+    rows, members, _ = fields[0].shape
     mine = lax.axis_index("member")
     per = LANES // width
     slot = lax.broadcasted_iota(jnp.int32, (members, LANES), 1) // width
@@ -301,15 +295,28 @@
         q = owner_of(mine, s, n)
         start = pl.multiple_of(q * width // LANES * LANES, LANES)
         offset = q * width - start
-        for f in range(3):
-            source = height if f == 0 else wind.at[f - 1]
+        for f, field in enumerate(fields):
             for r in range(0, rows, per):
                 total = None
                 for i in range(per):
-                    line = source[r + i, :, pl.ds(start, LANES)]
+                    line = field[r + i, :, pl.ds(start, LANES)]
                     line = pltpu.roll(line, lax.rem(i * width - offset + LANES, LANES), 1)
                     total = line if total is None else jnp.where(slot == i, line, total)
                 out[:, pl.ds((f * rows + r) * width, LANES)] = total
+
+
+def pack_height_kernel(width, n, shifts, height, *outs):
+    owner_blocks(width, n, shifts, [height], outs)
+
+
+def pack_kernel(width, n, shifts, own, got_pair, got_cross, *refs):
+    *outs, wind = refs
+    pair, cross = halo_places(own.shape[1])
+    wind[...] = own[1:3]
+    for f in range(2):
+        wind[f, pl.ds(pair, HALO)] += got_pair[f]
+        wind[f, pl.ds(cross, HALO)] += got_cross[f]
+    owner_blocks(width, n, shifts, [wind.at[0], wind.at[1]], outs)
 
 
 def owner_of(mine, shift, n):
@@ -400,21 +407,18 @@
 
 
 def apply_kernel(n, shifts, early, rows, weights, *refs):
-    parts, late, (pair_in, cross_in), outs, whole = (
-        refs[: n - 1],
-        refs[n - 1],
-        refs[n : n + 2],
-        refs[n + 2 : 2 * n + 2],
-        refs[2 * n + 2],
-    )
+    heights, parts = refs[: n - 1], refs[n - 1 : 2 * n - 2]
+    late, pair_in, cross_in = refs[2 * n - 2 : 2 * n + 1]
+    outs, whole = refs[2 * n + 1 : 3 * n + 1], refs[3 * n + 1]
     local, cells = late.shape
     mine = lax.axis_index("member")
 
     def place(s):
         return pl.ds(pl.multiple_of(source_of(mine, s, n) * local, local), local)
 
-    for s, part in zip(shifts, parts):
-        whole[place(s), :] = part[...]
+    for s, height, part in zip(shifts, heights, parts):
+        whole[place(s), : cells // 3] = height[...]
+        whole[place(s), cells // 3 :] = part[...]
     at = place(early)
     whole[at, :] = late[...]
     edge = cells // 3 // rows * HALO
@@ -507,16 +511,26 @@
     seen = lax.all_to_all(seen, "member", split_axis=0, concat_axis=0, tiled=True)
     uv_cross = lax.ppermute(after(uv_cross, early_block), "lat", cross_lat)
     uv_pair = lax.ppermute(after(uv_pair, early_block), "lat", pair_lat)
+    heights = call(
+        functools.partial(pack_height_kernel, width, n_member, late),
+        ([(members, rows * width)] * (n_member - 1), []),
+        height,
+        name="pack_height",
+    )
     packed = call(
         functools.partial(pack_kernel, width, n_member, late),
-        ([(members, dense)] * (n_member - 1), [pltpu.VMEM((2, rows, members, lon), F32)]),
-        own, height, uv_pair, uv_cross,
+        ([(members, 2 * rows * width)] * (n_member - 1), [pltpu.VMEM((2, rows, members, lon), F32)]),
+        own, uv_pair, uv_cross,
         name="pack",
     )
-    parts = [packed[0]] + [
-        lax.ppermute(block, "member", swap_links(n_member, s))
-        for s, block in zip(late[1:], packed[1:])
-    ]
+
+    def to_owners(blocks):
+        return [blocks[0]] + [
+            lax.ppermute(block, "member", swap_links(n_member, s))
+            for s, block in zip(late[1:], blocks[1:])
+        ]
+
+    heights, parts = to_owners(heights), to_owners(packed)
     beside = (members, 3 * HALO * width)
     early_own, early_pair, early_cross = call(
         functools.partial(owner_model_kernel, width, n_member, rows),
@@ -541,7 +555,7 @@
     )
     gram_cross = lax.ppermute(gram_cross, "lat", cross_lat)
     gram_pair = lax.ppermute(gram_pair, "lat", pair_lat)
-    raw_cross, raw_pair = lax.optimization_barrier((raw_cross, raw_pair, early_cross, early_pair))[:2]
+    raw_cross, raw_pair = lax.optimization_barrier((raw_cross, raw_pair, early_cross, early_pair, *heights))[:2]
     (gram_own,) = call(
         functools.partial(gram_kernel, (0,), *sizes),
         ([gram_shape], []),
@@ -558,11 +572,11 @@
     done = call(
         functools.partial(apply_kernel, n_member, late, early, rows),
         ([shape] * n_member, [pltpu.VMEM((all_members, dense), F32)]),
-        weights, *parts, early_own, early_pair, early_cross,
+        weights, *heights, *parts, early_own, early_pair, early_cross,
         name="apply", flops=6 * all_members**2 * dense,
     )
     final = [done[0]] + [None] * (n_member - 1)
-    for s in order:
+    for s in sorted(range(1, n_member), key=lambda s: (s != early, -s)):
         back = [(j, i) for i, j in swap_links(n_member, s)]
         final[s] = lax.ppermute(done[s], "member", back)
     (analysis,) = call(

time: 108 us -> 107 us (level)
    ppermute x1, starting transfers between devices: 5.92 us -> 3.03 us  [body(): gram_cross = lax.ppermute(gram_cross, 'lat', cross_lat)]
    ppermute x2 -> x4, starting transfers between devices: 3.52 us -> 6.4 us  [to_owners(): lax.ppermute(block, 'member', swap_links(n_member, s))]
    ppermute x3, waiting for transfers between devices: 32.9 us -> 34.1 us  [body(): final[s] = lax.ppermute(done[s], 'member', back)]
    pallas_call x10 -> x11, Pallas kernels: 21.7 us -> 21.9 us  [call(): pl.pallas_call(kernel, out_shape=shapes, in_specs=[pl.BlockSpec(memory_sp...]
  transfers between devices with their start and end apart: 17 -> 19, of which waited for: 8 -> 7; matrix products, arithmetic and copies ran while one was open for 0% -> 0% of each run, Pallas kernels for 16% -> 16%
where the time goes in v3:
time: 107 us
  waiting for transfers between devices  47.4 us (44%)
  starting transfers between devices  32.4 us (30%)
  Pallas kernels  21.9 us (20%)
  local copies, waits for them, and re-layouts  4.72 us (4%)
    ppermute x3, waiting for transfers between devices, body(): final[s] = lax.ppermute(done[s], 'member', back)  34.1 us
    pallas_call x11, Pallas kernels, call(): pl.pallas_call(kernel, out_shape=shapes, in_specs=[pl.BlockSpec(memory_sp...  21.9 us
    ppermute x1, waiting for transfers between devices, body(): got_cross = lax.ppermute(h_cross, 'lat', cross_lat)  7.74 us
    ppermute x4, starting transfers between devices, to_owners(): lax.ppermute(block, 'member', swap_links(n_member, s))  6.4 us
    unnamed x18, local copies, waits for them, and re-layouts  4.72 us
    ppermute x1, starting transfers between devices, body(): uv_cross = lax.ppermute(after(uv_cross, early_block), 'lat', cross_lat)  3.9 us
    all_to_all x1, starting transfers between devices, body(): lax.all_to_all(seen, 'member', split_axis=0, concat_axis=0, tiled=True)  3.82 us
    ppermute x1, starting transfers between devices, body(): early_cross = lax.ppermute(early_cross, 'lat', cross_lat)  3.62 us
  transfers between devices with their start and end apart: 19, of which 7 were waited for; matrix products, arithmetic and copies ran while one was open for 0% of the time, Pallas kernels for 16%

profile of v3, /device:TPU:11, one launch (start us, length us, event | category | flops | bytes accessed | tf_op | source)
XLA Modules:
  0.0 106.8 jit_solution(18212382358365731928)
XLA Ops:
  0.0 0.0 copy-start
  0.0 1.4 %copy-done = f32[3,64,8,256]{3,2,1,0:T(8,128)S(1)} copy-done((f32[3,64,8,256]{3,2,1,0:T(8,128)S(1)}, f32[3,64,8,256]{3,2,1,0:T(8,128)}, u32[]{:S(2)}) %copy-start) | copy-done | bytes 1572888
  1.4 0.0 copy-start.3
  1.4 1.2 %early.1 = f32[64,1792]{1,0:T(8,128)S(1)} custom-call(f32[3,1024,128]{2,1,0:T(8,128)S(1)} %bitcast.11), custom_call_target="tpu_custom_call" | custom-call | tf_op jit(solution)/shard_map/early/pallas_call | solution.py:27
  2.6 2.3 %collective-permute-start.2 = (f32[64,1792]{1,0:T(8,128)S(1)}, f32[64,1792]{1,0:T(8,128)S(1)}, u32[]{:S(2)}, u32[]{:S(2)}) collective-permute-start(f32[64,1792]{1,0:T(8,128)S(1)} %early.1), channel_id=1, source_target_pairs={{0,16},{8,24},{16,0},{24,8},{1,17},{9,25},{17,1},{25,9},{2,18},{10... | collective-permute-start | bytes 1376264 | tf_op jit(solution)/shard_map/ppermute | solution.py:495
  4.9 3.1 %model.1 = (f32[3,8,64,256]{3,2,1,0:T(8,128)S(1)}, f32[4,64,256]{2,1,0:T(8,128)S(1)}, f32[4,64,256]{2,1,0:T(8,128)S(1)}, f32[2,4,64,256]{3,2,1,0:T(8,128)S(1)}, f32[2,4,64,256]{3,2,1,0:T(8,128)S(1)}) custom-call(f32[3,1024,128]{2,1,0:T(8,128)S(1)} %bitcast.12), custom_call_target="tpu_custom_call" | custom-call | tf_op jit(solution)/shard_map/model/pallas_call | solution.py:27
  8.1 0.0 copy-start.8
  8.1 0.8 copy-done.8
  8.9 1.0 collective-permute-start
  9.8 3.0 %collective-permute-start.1 = (f32[4,64,256]{2,1,0:T(8,128)S(1)}, f32[4,64,256]{2,1,0:T(8,128)S(1)}, u32[]{:S(2)}, u32[]{:S(2)}) collective-permute-start(f32[4,64,256]{2,1,0:T(8,128)S(1)} %get-tuple-element.38), channel_id=1, source_target_pairs={{1,2},{3,4},{5,6},{2,1},{4,3},{6,5},{9,10},{11,12},{13,14},{10,9},... | collective-permute-start | bytes 786440 | tf_op jit(solution)/shard_map/ppermute | solution.py:503
  12.8 0.0 collective-permute-done.got_pair
  12.8 7.7 %collective-permute-done.1.got_cross = f32[4,64,256]{2,1,0:T(8,128)S(1)} collective-permute-done((f32[4,64,256]{2,1,0:T(8,128)S(1)}, f32[4,64,256]{2,1,0:T(8,128)S(1)}, u32[]{:S(2)}, u32[]{:S(2)}) %collective-permute-start.1) | collective-permute-done | bytes 262176 | tf_op jit(solution)/shard_map/ppermute | solution.py:503
  20.6 0.0 copy-done.3
  20.6 0.8 observe.1
  21.4 0.0 copy-done.7
  21.4 0.0 copy-start.4
  21.4 0.7 copy-done.4
  22.1 3.8 %all-to-all-start = ((f32[4,64,256]{2,1,0:T(8,128)}), f32[4,64,256]{2,1,0:T(8,128)S(1)}, u32[]{:S(2)}, u32[]{:S(2)}) async-start(f32[4,64,256]{2,1,0:T(8,128)} %copy-done.4), calls=%async_computation | async-start | bytes 524288 | tf_op jit(solution)/shard_map/all_to_all | solution.py:511
  25.9 0.0 collective-permute-done.2.block_in
  25.9 0.8 copy-done.1
  26.7 0.0 collective-permute-start.5
  26.7 3.9 %collective-permute-start.6 = (f32[2,4,64,256]{3,2,1,0:T(8,128)}, f32[2,4,64,256]{3,2,1,0:T(8,128)S(1)}, u32[]{:S(2)}, u32[]{:S(2)}) collective-permute-start(f32[2,4,64,256]{3,2,1,0:T(8,128)} %copy-done.7), channel_id=1, source_target_pairs={{1,2},{3,4},{5,6},{2,1},{4,3},{6,5},{9,10},{11,12},{13,14},{10,9},... | collective-permute-start | bytes 1572872 | tf_op jit(solution)/shard_map/ppermute | solution.py:512
  30.6 1.3 %all-to-all-done = f32[4,64,256]{2,1,0:T(8,128)S(1)} async-done(((f32[4,64,256]{2,1,0:T(8,128)}), f32[4,64,256]{2,1,0:T(8,128)S(1)}, u32[]{:S(2)}, u32[]{:S(2)}) %all-to-all-start) | async-done | bytes 262176 | tf_op jit(solution)/shard_map/all_to_all | solution.py:511
  31.9 2.0 %collective-permute-start.3 = (f32[256,256]{1,0:T(8,128)S(1)}, f32[256,256]{1,0:T(8,128)S(1)}, u32[]{:S(2)}, u32[]{:S(2)}) collective-permute-start(f32[256,256]{1,0:T(8,128)S(1)} %bitcast.13), channel_id=1, source_target_pairs={{8,16},{16,8},{9,17},{17,9},{10,18},{18,10},{11,19},{19,11},{12,20... | collective-permute-start | bytes 786440 | tf_op jit(solution)/shard_map/ppermute | solution.py:544
  33.8 0.3 collective-permute-start.4
  34.1 1.0 copy-done.2
  35.2 3.3 %owner_model.1 = (f32[64,1536]{1,0:T(8,128)S(1)}, f32[64,768]{1,0:T(8,128)S(1)}, f32[64,768]{1,0:T(8,128)S(1)}) custom-call(f32[64,1792]{1,0:T(8,128)S(1)} %copy-done.2), custom_call_target="tpu_custom_call" | custom-call | tf_op jit(solution)/shard_map/owner_model/pallas_call | solution.py:27
  38.5 3.6 %collective-permute-start.7 = (f32[64,768]{1,0:T(8,128)S(1)}, f32[64,768]{1,0:T(8,128)S(1)}, u32[]{:S(2)}, u32[]{:S(2)}) collective-permute-start(f32[64,768]{1,0:T(8,128)S(1)} %get-tuple-element.51), channel_id=1, source_target_pairs={{1,2},{3,4},{5,6},{2,1},{4,3},{6,5},{9,10},{11,12},{13,14},{10,9},... | collective-permute-start | bytes 589832 | tf_op jit(solution)/shard_map/ppermute | solution.py:541
  42.1 0.0 copy-start.5
  42.1 0.0 copy-start.6
  42.1 0.3 pack_height.1
  42.4 0.0 collective-permute-done.5.got_pair
  42.4 1.5 %collective-permute-start.10 = (f32[64,512]{1,0:T(8,128)S(1)}, f32[64,512]{1,0:T(8,128)S(1)}, u32[]{:S(2)}, u32[]{:S(2)}) collective-permute-start(f32[64,512]{1,0:T(8,128)S(1)} %get-tuple-element.56), channel_id=1, source_target_pairs={{0,24},{8,16},{16,8},{24,0},{1,25},{9,17},{17,9},{25,1},{2,26},{10... | collective-permute-start | bytes 393224 | tf_op jit(solution)/shard_map/ppermute | solution.py:529
  43.9 0.0 collective-permute-done.6.got_cross
  43.9 2.6 %collective-permute-start.9 = (f32[64,512]{1,0:T(8,128)S(1)}, f32[64,512]{1,0:T(8,128)S(1)}, u32[]{:S(2)}, u32[]{:S(2)}) collective-permute-start(f32[64,512]{1,0:T(8,128)S(1)} %get-tuple-element.55), channel_id=1, source_target_pairs={{0,8},{8,0},{16,24},{24,16},{1,9},{9,1},{17,25},{25,17},{2,10},{10... | collective-permute-start | bytes 393224 | tf_op jit(solution)/shard_map/ppermute | solution.py:529
  46.6 0.6 pack.1
  47.2 0.0 collective-permute-done.3.raw_cross
  47.2 0.0 collective-permute-done.4.raw_pair
  47.2 0.0 copy-done.5
  47.3 0.0 copy-done.6
  47.3 0.9 gram_beside.1
  48.2 0.1 collective-permute-start.11
  48.3 3.0 %collective-permute-start.12 = (f32[272,256]{1,0:T(8,128)S(1)}, f32[272,256]{1,0:T(8,128)S(1)}, u32[]{:S(2)}, u32[]{:S(2)}) collective-permute-start(f32[272,256]{1,0:T(8,128)S(1)} %get-tuple-element.60), channel_id=1, source_target_pairs={{1,2},{3,4},{5,6},{2,1},{4,3},{6,5},{9,10},{11,12},{13,14},{10,9},... | collective-permute-start | bytes 835592 | tf_op jit(solution)/shard_map/ppermute | solution.py:556
  51.3 0.0 collective-permute-done.10.refs_2_
  51.3 0.2 collective-permute-start.13
  51.5 0.0 collective-permute-done.9.refs_1_
  51.5 2.1 %collective-permute-start.14 = (f32[64,1024]{1,0:T(8,128)S(1)}, f32[64,1024]{1,0:T(8,128)S(1)}, u32[]{:S(2)}, u32[]{:S(2)}) collective-permute-start(f32[64,1024]{1,0:T(8,128)S(1)} %get-tuple-element.47), channel_id=1, source_target_pairs={{0,24},{8,16},{16,8},{24,0},{1,25},{9,17},{17,9},{25,1},{2,26},{10... | collective-permute-start | bytes 786440 | tf_op jit(solution)/shard_map/ppermute | solution.py:529
  53.6 0.0 collective-permute-done.7.refs_8_
  53.6 0.0 collective-permute-start.8
  53.6 1.4 %collective-permute-done.8.refs_7_ = f32[64,768]{1,0:T(8,128)S(1)} collective-permute-done((f32[64,768]{1,0:T(8,128)S(1)}, f32[64,768]{1,0:T(8,128)S(1)}, u32[]{:S(2)}, u32[]{:S(2)}) %collective-permute-start.8) | collective-permute-done | bytes 196640 | tf_op jit(solution)/shard_map/ppermute | solution.py:542
  55.0 0.6 gram_own.1.own
  55.6 0.0 collective-permute-done.11.got_pair
  55.6 2.9 %collective-permute-done.12.got_cross = f32[272,256]{1,0:T(8,128)S(1)} collective-permute-done((f32[272,256]{1,0:T(8,128)S(1)}, f32[272,256]{1,0:T(8,128)S(1)}, u32[]{:S(2)}, u32[]{:S(2)}) %collective-permute-start.12) | collective-permute-done | bytes 278560 | tf_op jit(solution)/shard_map/ppermute | solution.py:556
  58.5 8.0 %weights.1 = f32[256,256]{1,0:T(8,128)S(1)} custom-call(f32[272,256]{1,0:T(8,128)S(1)} %gram_own.1.own, f32[272,256]{1,0:T(8,128)S(1)} %collective-permute-done.11.got_pair, f32[272,256]{1,0:T(8,128)S(1)} %collective-permute-done.12.got_cross), custom_call_target="tpu_custom_call" | custom-call | tf_op jit(solution)/shard_map/weights/pallas_call | solution.py:27
  66.5 0.0 collective-permute-done.13.refs_4_
  66.5 0.0 collective-permute-done.14.refs_5_
  66.5 1.3 %apply.1 = (f32[64,1536]{1,0:T(8,128)S(1)}, f32[64,1536]{1,0:T(8,128)S(1)}, f32[64,1536]{1,0:T(8,128)S(1)}, f32[64,1536]{1,0:T(8,128)S(1)}) custom-call(f32[256,256]{1,0:T(8,128)S(1)} %weights.1, f32[64,512]{1,0:T(8,128)S(1)} %get-tuple-element.54.refs_0_, f32[64,512]{1,0:T(8,128)S(1)} %collective-permute-done.9.refs_1_, ...), custom_call_target="tpu_custom_call" | custom-call | tf_op jit(solution)/shard_map/apply/pallas_call | solution.py:27
  67.8 0.5 collective-permute-start.15
  68.3 2.5 %collective-permute-start.16 = (f32[64,1536]{1,0:T(8,128)S(1)}, f32[64,1536]{1,0:T(8,128)S(1)}, u32[]{:S(2)}, u32[]{:S(2)}) collective-permute-start(f32[64,1536]{1,0:T(8,128)S(1)} %get-tuple-element.63), channel_id=1, source_target_pairs={{16,0},{24,8},{0,16},{8,24},{17,1},{25,9},{1,17},{9,25},{18,2},{26... | collective-permute-start | bytes 1179656 | tf_op jit(solution)/shard_map/ppermute | solution.py:581
  70.8 0.0 collective-permute-start.17
  70.8 14.2 %collective-permute-done.15.refs_1_ = f32[64,1536]{1,0:T(8,128)S(1)} collective-permute-done((f32[64,1536]{1,0:T(8,128)S(1)}, f32[64,1536]{1,0:T(8,128)S(1)}, u32[]{:S(2)}, u32[]{:S(2)}) %collective-permute-start.15) | collective-permute-done | bytes 393248 | tf_op jit(solution)/shard_map/ppermute | solution.py:581
  85.0 11.6 %collective-permute-done.16.refs_2_ = f32[64,1536]{1,0:T(8,128)S(1)} collective-permute-done((f32[64,1536]{1,0:T(8,128)S(1)}, f32[64,1536]{1,0:T(8,128)S(1)}, u32[]{:S(2)}, u32[]{:S(2)}) %collective-permute-start.16) | collective-permute-done | bytes 393248 | tf_op jit(solution)/shard_map/ppermute | solution.py:581
  96.6 8.3 %collective-permute-done.17.refs_3_ = f32[64,1536]{1,0:T(8,128)S(1)} collective-permute-done((f32[64,1536]{1,0:T(8,128)S(1)}, f32[64,1536]{1,0:T(8,128)S(1)}, u32[]{:S(2)}, u32[]{:S(2)}) %collective-permute-start.17) | collective-permute-done | bytes 393248 | tf_op jit(solution)/shard_map/ppermute | solution.py:581
  104.9 1.8 %unpack.1 = f32[3,1024,128]{2,1,0:T(8,128)} custom-call(f32[64,1536]{1,0:T(8,128)S(1)} %get-tuple-element.61.refs_0_, f32[64,1536]{1,0:T(8,128)S(1)} %collective-permute-done.15.refs_1_, f32[64,1536]{1,0:T(8,128)S(1)} %collective-permute-done.16.refs_2_, f32[64,1536]{1,0:T(8,128)S(1)} %collective-permute-done.17.refs_3_), custom_call_target="tpu_custom_call" | custom-call | tf_op jit(solution)/shard_map/unpack/pallas_call | solution.py:27
  (3 shorter events, 0.0 us)
Async XLA Ops:
  0.0 1.4 %copy-start = (f32[3,64,8,256]{3,2,1,0:T(8,128)S(1)}, f32[3,64,8,256]{3,2,1,0:T(8,128)}, u32[]{:S(2)}) copy-start(f32[3,64,8,256]{3,2,1,0:T(8,128)} %param.4) | copy-start | bytes 4718596
  1.4 19.2 %copy-start.3 = (s32[8,4,256]{2,1,0:T(4,128)S(1)}, s32[8,4,256]{2,1,0:T(4,128)}, u32[]{:S(2)}) copy-start(s32[8,4,256]{2,1,0:T(4,128)} %cells.5) | copy-start | bytes 98308
  2.6 23.3 %collective-permute-start.2 = (f32[64,1792]{1,0:T(8,128)S(1)}, f32[64,1792]{1,0:T(8,128)S(1)}, u32[]{:S(2)}, u32[]{:S(2)}) collective-permute-start(f32[64,1792]{1,0:T(8,128)S(1)} %early.1), channel_id=1, source_target_pairs={{0,16},{8,24},{16,0},{24,8},{1,17},{9,25},{17,1},{25,9},{2,18},{10... | collective-permute-start | bytes 1376264 | tf_op jit(solution)/shard_map/ppermute | solution.py:495
  8.1 0.8 copy-start.8
  8.9 12.5 %copy-start.7 = (f32[2,4,64,256]{3,2,1,0:T(8,128)}, f32[2,4,64,256]{3,2,1,0:T(8,128)S(1)}, u32[]{:S(2)}) copy-start(f32[2,4,64,256]{3,2,1,0:T(8,128)S(1)} %get-tuple-element.44) | copy-start | bytes 1572868
  8.9 4.0 %collective-permute-start = (f32[4,64,256]{2,1,0:T(8,128)S(1)}, f32[4,64,256]{2,1,0:T(8,128)S(1)}, u32[]{:S(2)}, u32[]{:S(2)}) collective-permute-start(f32[4,64,256]{2,1,0:T(8,128)S(1)} %get-tuple-element.37), channel_id=1, source_target_pairs={{0,1},{2,3},{4,5},{6,7},{1,0},{3,2},{5,4},{7,6},{8,9},{10,11},{12,... | collective-permute-start | bytes 786440 | tf_op jit(solution)/shard_map/ppermute | solution.py:504
  9.8 10.8 %collective-permute-start.1 = (f32[4,64,256]{2,1,0:T(8,128)S(1)}, f32[4,64,256]{2,1,0:T(8,128)S(1)}, u32[]{:S(2)}, u32[]{:S(2)}) collective-permute-start(f32[4,64,256]{2,1,0:T(8,128)S(1)} %get-tuple-element.38), channel_id=1, source_target_pairs={{1,2},{3,4},{5,6},{2,1},{4,3},{6,5},{9,10},{11,12},{13,14},{10,9},... | collective-permute-start | bytes 786440 | tf_op jit(solution)/shard_map/ppermute | solution.py:503
  21.4 0.7 copy-start.4
  22.1 9.8 %all-to-all-start = ((f32[4,64,256]{2,1,0:T(8,128)}), f32[4,64,256]{2,1,0:T(8,128)S(1)}, u32[]{:S(2)}, u32[]{:S(2)}) async-start(f32[4,64,256]{2,1,0:T(8,128)} %copy-done.4), calls=%async_computation | async-start | bytes 524288 | tf_op jit(solution)/shard_map/all_to_all | solution.py:511
  25.9 0.8 copy-start.1
  26.7 15.7 %collective-permute-start.5 = (f32[2,4,64,256]{3,2,1,0:T(8,128)}, f32[2,4,64,256]{3,2,1,0:T(8,128)S(1)}, u32[]{:S(2)}, u32[]{:S(2)}) collective-permute-start(f32[2,4,64,256]{3,2,1,0:T(8,128)} %copy-done.8), channel_id=1, source_target_pairs={{0,1},{2,3},{4,5},{6,7},{1,0},{3,2},{5,4},{7,6},{8,9},{10,11},{12,... | collective-permute-start | bytes 1572872 | tf_op jit(solution)/shard_map/ppermute | solution.py:513
  26.7 17.2 %collective-permute-start.6 = (f32[2,4,64,256]{3,2,1,0:T(8,128)}, f32[2,4,64,256]{3,2,1,0:T(8,128)S(1)}, u32[]{:S(2)}, u32[]{:S(2)}) collective-permute-start(f32[2,4,64,256]{3,2,1,0:T(8,128)} %copy-done.7), channel_id=1, source_target_pairs={{1,2},{3,4},{5,6},{2,1},{4,3},{6,5},{9,10},{11,12},{13,14},{10,9},... | collective-permute-start | bytes 1572872 | tf_op jit(solution)/shard_map/ppermute | solution.py:512
  31.9 15.4 %collective-permute-start.3 = (f32[256,256]{1,0:T(8,128)S(1)}, f32[256,256]{1,0:T(8,128)S(1)}, u32[]{:S(2)}, u32[]{:S(2)}) collective-permute-start(f32[256,256]{1,0:T(8,128)S(1)} %bitcast.13), channel_id=1, source_target_pairs={{8,16},{16,8},{9,17},{17,9},{10,18},{18,10},{11,19},{19,11},{12,20... | collective-permute-start | bytes 786440 | tf_op jit(solution)/shard_map/ppermute | solution.py:544
  33.8 13.4 %collective-permute-start.4 = (f32[256,256]{1,0:T(8,128)S(1)}, f32[256,256]{1,0:T(8,128)S(1)}, u32[]{:S(2)}, u32[]{:S(2)}) collective-permute-start(f32[256,256]{1,0:T(8,128)S(1)} %bitcast.14), channel_id=1, source_target_pairs={{0,8},{16,24},{8,0},{24,16},{1,9},{17,25},{9,1},{25,17},{2,10},{18... | collective-permute-start | bytes 786440 | tf_op jit(solution)/shard_map/ppermute | solution.py:545
  34.1 1.0 copy-start.2
  38.5 15.1 %collective-permute-start.7 = (f32[64,768]{1,0:T(8,128)S(1)}, f32[64,768]{1,0:T(8,128)S(1)}, u32[]{:S(2)}, u32[]{:S(2)}) collective-permute-start(f32[64,768]{1,0:T(8,128)S(1)} %get-tuple-element.51), channel_id=1, source_target_pairs={{1,2},{3,4},{5,6},{2,1},{4,3},{6,5},{9,10},{11,12},{13,14},{10,9},... | collective-permute-start | bytes 589832 | tf_op jit(solution)/shard_map/ppermute | solution.py:541
  42.1 5.1 %copy-start.5 = (f32[8,4,256]{2,1,0:T(4,128)S(1)}, f32[8,4,256]{2,1,0:T(4,128)}, u32[]{:S(2)}) copy-start(f32[8,4,256]{2,1,0:T(4,128)} %values.3) | copy-start | bytes 98308
  42.1 5.1 %copy-start.6 = (f32[8,4,256]{2,1,0:T(4,128)S(1)}, f32[8,4,256]{2,1,0:T(4,128)}, u32[]{:S(2)}) copy-start(f32[8,4,256]{2,1,0:T(4,128)} %precs.3) | copy-start | bytes 98308
  42.4 8.9 %collective-permute-start.10 = (f32[64,512]{1,0:T(8,128)S(1)}, f32[64,512]{1,0:T(8,128)S(1)}, u32[]{:S(2)}, u32[]{:S(2)}) collective-permute-start(f32[64,512]{1,0:T(8,128)S(1)} %get-tuple-element.56), channel_id=1, source_target_pairs={{0,24},{8,16},{16,8},{24,0},{1,25},{9,17},{17,9},{25,1},{2,26},{10... | collective-permute-start | bytes 393224 | tf_op jit(solution)/shard_map/ppermute | solution.py:529
  43.9 7.6 %collective-permute-start.9 = (f32[64,512]{1,0:T(8,128)S(1)}, f32[64,512]{1,0:T(8,128)S(1)}, u32[]{:S(2)}, u32[]{:S(2)}) collective-permute-start(f32[64,512]{1,0:T(8,128)S(1)} %get-tuple-element.55), channel_id=1, source_target_pairs={{0,8},{8,0},{16,24},{24,16},{1,9},{9,1},{17,25},{25,17},{2,10},{10... | collective-permute-start | bytes 393224 | tf_op jit(solution)/shard_map/ppermute | solution.py:529
  48.2 7.4 %collective-permute-start.11 = (f32[272,256]{1,0:T(8,128)S(1)}, f32[272,256]{1,0:T(8,128)S(1)}, u32[]{:S(2)}, u32[]{:S(2)}) collective-permute-start(f32[272,256]{1,0:T(8,128)S(1)} %get-tuple-element.59), channel_id=1, source_target_pairs={{0,1},{2,3},{4,5},{6,7},{1,0},{3,2},{5,4},{7,6},{8,9},{10,11},{12,... | collective-permute-start | bytes 835592 | tf_op jit(solution)/shard_map/ppermute | solution.py:557
  48.3 10.2 %collective-permute-start.12 = (f32[272,256]{1,0:T(8,128)S(1)}, f32[272,256]{1,0:T(8,128)S(1)}, u32[]{:S(2)}, u32[]{:S(2)}) collective-permute-start(f32[272,256]{1,0:T(8,128)S(1)} %get-tuple-element.60), channel_id=1, source_target_pairs={{1,2},{3,4},{5,6},{2,1},{4,3},{6,5},{9,10},{11,12},{13,14},{10,9},... | collective-permute-start | bytes 835592 | tf_op jit(solution)/shard_map/ppermute | solution.py:556
  51.3 15.2 %collective-permute-start.13 = (f32[64,1024]{1,0:T(8,128)S(1)}, f32[64,1024]{1,0:T(8,128)S(1)}, u32[]{:S(2)}, u32[]{:S(2)}) collective-permute-start(f32[64,1024]{1,0:T(8,128)S(1)} %get-tuple-element.46), channel_id=1, source_target_pairs={{0,8},{8,0},{16,24},{24,16},{1,9},{9,1},{17,25},{25,17},{2,10},{10... | collective-permute-start | bytes 786440 | tf_op jit(solution)/shard_map/ppermute | solution.py:529
  51.5 15.0 %collective-permute-start.14 = (f32[64,1024]{1,0:T(8,128)S(1)}, f32[64,1024]{1,0:T(8,128)S(1)}, u32[]{:S(2)}, u32[]{:S(2)}) collective-permute-start(f32[64,1024]{1,0:T(8,128)S(1)} %get-tuple-element.47), channel_id=1, source_target_pairs={{0,24},{8,16},{16,8},{24,0},{1,25},{9,17},{17,9},{25,1},{2,26},{10... | collective-permute-start | bytes 786440 | tf_op jit(solution)/shard_map/ppermute | solution.py:529
  53.6 1.4 %collective-permute-start.8 = (f32[64,768]{1,0:T(8,128)S(1)}, f32[64,768]{1,0:T(8,128)S(1)}, u32[]{:S(2)}, u32[]{:S(2)}) collective-permute-start(f32[64,768]{1,0:T(8,128)S(1)} %get-tuple-element.52), channel_id=1, source_target_pairs={{0,1},{2,3},{4,5},{6,7},{1,0},{3,2},{5,4},{7,6},{8,9},{10,11},{12,... | collective-permute-start | bytes 589832 | tf_op jit(solution)/shard_map/ppermute | solution.py:542
  67.8 17.1 %collective-permute-start.15 = (f32[64,1536]{1,0:T(8,128)S(1)}, f32[64,1536]{1,0:T(8,128)S(1)}, u32[]{:S(2)}, u32[]{:S(2)}) collective-permute-start(f32[64,1536]{1,0:T(8,128)S(1)} %get-tuple-element.62), channel_id=1, source_target_pairs={{8,0},{0,8},{24,16},{16,24},{9,1},{1,9},{25,17},{17,25},{10,2},{2,... | collective-permute-start | bytes 1179656 | tf_op jit(solution)/shard_map/ppermute | solution.py:581
  68.3 28.3 %collective-permute-start.16 = (f32[64,1536]{1,0:T(8,128)S(1)}, f32[64,1536]{1,0:T(8,128)S(1)}, u32[]{:S(2)}, u32[]{:S(2)}) collective-permute-start(f32[64,1536]{1,0:T(8,128)S(1)} %get-tuple-element.63), channel_id=1, source_target_pairs={{16,0},{24,8},{0,16},{8,24},{17,1},{25,9},{1,17},{9,25},{18,2},{26... | collective-permute-start | bytes 1179656 | tf_op jit(solution)/shard_map/ppermute | solution.py:581
  70.8 34.1 %collective-permute-start.17 = (f32[64,1536]{1,0:T(8,128)S(1)}, f32[64,1536]{1,0:T(8,128)S(1)}, u32[]{:S(2)}, u32[]{:S(2)}) collective-permute-start(f32[64,1536]{1,0:T(8,128)S(1)} %get-tuple-element.64), channel_id=1, source_target_pairs={{24,0},{16,8},{8,16},{0,24},{25,1},{17,9},{9,17},{1,25},{26,2},{18... | collective-permute-start | bytes 1179656 | tf_op jit(solution)/shard_map/ppermute | solution.py:581
